TPU v7x, 256 devices: a whole 4x4x8 slice. The times are simulated.
256 devices in a mesh: inst: 32 (over y, x, z_lo), tp: 8 (over z_hi, core).
Axes of the slice: x: 4, y: 4, z: 8 (z_hi: 4, z_lo: 2; z = z_hi * 2 + z_lo), core: 2. Of those that a mesh axis runs over, the one named last changes fastest.
Arguments:
- pool: bfloat16 [1536, 2, 128, 1024], P('inst', None, None, 'tp'), may hold values from -8 to 8
- page_table: int32 [1024, 2], P('inst'), may hold values from 0 to 47, as said below
- lengths: int32 [1024], P('inst'), may hold values from 1 to 253
- targets: int32 [1024], P('inst'), may hold values from 0 to 31, as said below
- migrating: int32 [1024], P('inst'), may hold values 0 or 1
- queries_src: bfloat16 [1024, 2, 4096], P('inst', None, 'tp'), may hold values from -6 to 6
- new_rows: bfloat16 [1024, 2, 2, 1024], P('inst', None, None, 'tp'), may hold values from -6 to 6
- queries_dst: bfloat16 [1024, 4096], P('inst', 'tp'), may hold values from -6 to 6
- rows_dst: bfloat16 [1024, 2, 1024], P('inst', None, 'tp'), may hold values from -6 to 6
- w_out: bfloat16 [4096, 4096], P('tp'), may hold values from -1 to 1
Outputs:
- src_out: bfloat16 [1024, 2, 4096], P('inst')
- dest_cache: bfloat16 [1024, 2, 2, 128, 1024], P('inst', None, None, None, 'tp')
- dst_out: bfloat16 [1024, 4096], P('inst')
Inputs may be any that keep to these rules, and one draw needn't show every extreme that they name: `page_table`: the first ceil(lengths / 128) entries of a request name pages of its instance's pool that no other request names; the pages of an instance's 32 requests fill its 48 pool pages exactly; later entries are valid page numbers. `targets`: every destination is named by exactly 1 of the 32 requests of each source instance.
All inputs are finite; a program needn't handle non-finite values. No bound on the sum of `migrating` on one device may be relied on, other than what follows from the above.
Results may differ from a plain program's by a relative error of at most 0.0058.
Values may be sent and summed in bfloat16 or wider, within the bound.
A program may use at most 128 MiB of HBM per device.

v0:
```python
from functools import reduce
import math

import jax
import jax.numpy as jnp
from jax import lax
from jax.sharding import PartitionSpec as P

KVH = 8


masked_score = -1e30


def attend(query_heads, blocks):
    scale = 1.0 / math.sqrt(query_heads.shape[-1])
    scored = []
    for block_keys, block_values, block_keep in blocks:
        raw_scores = (
            jnp.einsum(
                "bthge,bshe->bthgs", query_heads, block_keys, preferred_element_type=jnp.float32
            )
            * scale
        )
        scored.append(jnp.where(block_keep[:, :, None, None, :], raw_scores, masked_score))
    highest = reduce(jnp.maximum, [jnp.max(entry, axis=-1, keepdims=True) for entry in scored])
    powers = [jnp.exp(entry - highest) for entry in scored]
    totals = reduce(jnp.add, [jnp.sum(entry, axis=-1, keepdims=True) for entry in powers])
    mixed = jnp.zeros(query_heads.shape, jnp.float32)
    for weight_block, block in zip(powers, blocks):
        weights = (weight_block / totals).astype(jnp.bfloat16)
        mixed = mixed + jnp.einsum(
            "bthgs,bshe->bthge", weights, block[1], preferred_element_type=jnp.float32
        )
    return mixed.astype(jnp.bfloat16)


def shards(
    pool,
    page_table,
    lengths,
    targets,
    migrating,
    queries_src,
    new_rows,
    queries_dst,
    rows_dst,
    w_out,
):
    requests, steps, width = queries_src.shape
    pages = page_table.shape[1]
    page_rows = pool.shape[2]
    kv_width = pool.shape[3]
    heads_local = KVH // lax.axis_size("tp")
    head_size = kv_width // heads_local
    groups = width // kv_width
    span = pages * page_rows
    instances = lax.axis_size("inst")
    per_pair = requests // instances
    zero_value = jnp.zeros((), jnp.bfloat16)
    position = jnp.arange(span, dtype=jnp.int32)
    page_grid = (
        jnp.arange(pages, dtype=jnp.int32)[:, None] * page_rows
        + jnp.arange(page_rows, dtype=jnp.int32)[None, :]
    )
    ordinal = jnp.arange(requests, dtype=jnp.int32)
    view = pool[page_table]
    same_target = targets[:, None] == targets[None, :]
    rank_of = jnp.sum(
        (same_target & (ordinal[None, :] < ordinal[:, None])).astype(jnp.int32), axis=1
    )
    slot_of = targets * per_pair + rank_of
    inverse = jnp.sum(jnp.where(slot_of[:, None] == ordinal[None, :], ordinal[:, None], 0), axis=0)
    moving = migrating == 1
    held = moving[:, None, None] & (page_grid[None] < lengths[:, None, None])
    outgoing = jnp.where(held[:, :, None, :, None], view, zero_value)[inverse]
    outgoing = outgoing.reshape(instances, per_pair, pages, 2, page_rows, kv_width)
    fresh_out = jnp.where(moving[:, None, None, None], new_rows, zero_value)[inverse]
    fresh_out = fresh_out.reshape(instances, per_pair, steps, 2, kv_width)
    len_out = lengths[inverse].reshape(instances, per_pair)
    flag_out = migrating[inverse].reshape(instances, per_pair)
    fresh_in, len_in, flag_in = (
        lax.all_to_all(fresh_out, "inst", split_axis=0, concat_axis=0, tiled=True),
        lax.all_to_all(len_out, "inst", split_axis=0, concat_axis=0, tiled=True),
        lax.all_to_all(flag_out, "inst", split_axis=0, concat_axis=0, tiled=True),
    )
    arrived = lax.all_to_all(outgoing, "inst", split_axis=0, concat_axis=0, tiled=True)
    old_keys = view[:, :, 0].reshape(requests, span, heads_local, head_size)
    old_values = view[:, :, 1].reshape(requests, span, heads_local, head_size)
    keep_old = (position[None, :] < lengths[:, None])[:, None, :]
    fresh_keep = (jnp.arange(steps)[None, :] <= jnp.arange(steps)[:, None])[None]
    fresh_keys = new_rows[:, :, 0].reshape(requests, steps, heads_local, head_size)
    fresh_values = new_rows[:, :, 1].reshape(requests, steps, heads_local, head_size)
    query_src = queries_src.reshape(requests, steps, heads_local, groups, head_size)
    attended_src = attend(
        query_src, [(old_keys, old_values, keep_old), (fresh_keys, fresh_values, fresh_keep)]
    )
    partial_src = jnp.dot(
        attended_src.reshape(requests * steps, width), w_out, preferred_element_type=jnp.float32
    )
    arrived = arrived.reshape(requests, pages, 2, page_rows, kv_width)
    fresh_in = fresh_in.reshape(requests, steps, 2, kv_width)
    len_in = len_in.reshape(requests)
    flag_in = flag_in.reshape(requests)
    own_rows = jnp.where((flag_in == 1)[:, None, None], rows_dst, zero_value)
    offset = (page_grid[None] - len_in[:, None, None])[:, :, None, :, None]
    filled = jnp.where(offset == 0, fresh_in[:, 0][:, None, :, None, :], arrived)
    filled = jnp.where(offset == 1, fresh_in[:, 1][:, None, :, None, :], filled)
    filled = jnp.where(offset == 2, own_rows[:, None, :, None, :], filled)
    dst_keys = filled[:, :, 0].reshape(requests, span, heads_local, head_size)
    dst_values = filled[:, :, 1].reshape(requests, span, heads_local, head_size)
    keep_new = (position[None, :] < (len_in + 3)[:, None])[:, None, :]
    query_dst = queries_dst.reshape(requests, 1, heads_local, groups, head_size)
    attended_dst = attend(query_dst, [(dst_keys, dst_values, keep_new)])
    attended_dst = jnp.where((flag_in == 1)[:, None, None, None, None], attended_dst, zero_value)
    partial_dst = jnp.dot(
        attended_dst.reshape(requests, width), w_out, preferred_element_type=jnp.float32
    )
    src_total = lax.psum(partial_src, "tp").astype(jnp.bfloat16)
    dst_total = lax.psum(partial_dst, "tp").astype(jnp.bfloat16)
    return (src_total.reshape(requests, steps, -1), filled, dst_total)


def solution(mesh):
    return jax.shard_map(
        shards,
        mesh=mesh,
        in_specs=(
            P("inst", None, None, "tp"),
            P("inst", None),
            P("inst"),
            P("inst"),
            P("inst"),
            P("inst", None, "tp"),
            P("inst", None, None, "tp"),
            P("inst", "tp"),
            P("inst", None, "tp"),
            P("tp", None),
        ),
        out_specs=(P("inst", None, None), P("inst", None, None, None, "tp"), P("inst", None)),
        check_vma=False,
    )
```

profile of v0, /device:TPU:1, one launch (start us, length us, event | category | flops | bytes accessed | tf_op | source)
XLA Modules:
  0.0 192.9 jit_solution(10331995849464394775)
XLA Ops:
  0.6 0.0 copy-start
  0.6 1.0 convert_reduce_fusion
  1.6 0.7 add.79
  2.3 0.1 select_reduce_fusion
  2.4 1.4 gather_fusion.1
  3.8 0.7 copy.42
  4.5 9.2 %all-to-all-start = ((s32[32,1,1]{2,1,0:T(1,128)}), s32[32,1,1]{2,1,0:T(1,128)S(1)}, u32[]{:S(2)}, u32[]{:S(2)}) async-start(s32[32,1,1]{2,1,0:T(1,128)} %copy.42), calls=%async_computation | async-start | bytes 32768 | tf_op jit(solution)/shard_map/all_to_all | solution.py:84
  13.7 0.7 broadcast_compare_fusion
  14.4 1.4 gather_fusion.2
  15.7 0.7 compare_select_fusion
  16.4 0.1 copy.37
  16.5 0.1 reshape.284
  16.6 0.1 iota_add_fusion
  16.7 0.9 broadcast_select_fusion.1
  17.6 1.2 gather_fusion.3
  18.8 0.7 copy.43
  19.5 0.0 copy-done
  19.5 0.0 copy-start.1
  19.5 3.1 %gather_fusion = bf16[64,2,128,128]{3,2,1,0:T(8,128)(2,1)} fusion(bf16[48,2,128,128]{3,2,1,0:T(8,128)(2,1)S(1)} %copy-done, s32[1024]{0:T(1024)S(1)} %pad_clamp_fusion.1), kind=kCustom, calls=%fused_computation | custom fusion | bytes 8388864 | tf_op jit(solution)/shard_map/gather | solution.py:67
  22.6 0.0 all-to-all-done
  22.6 7.7 %all-to-all-start.1 = ((s32[32,1,1]{2,1,0:T(1,128)}), s32[32,1,1]{2,1,0:T(1,128)S(1)}, u32[]{:S(2)}, u32[]{:S(2)}) async-start(s32[32,1,1]{2,1,0:T(1,128)} %copy.43), calls=%async_computation.1 | async-start | bytes 32768 | tf_op jit(solution)/shard_map/all_to_all | solution.py:85
  30.3 0.7 reduce.6
  31.0 0.0 copy-done.1
  31.0 0.2 subtract_compare_fusion.2
  31.2 6.2 %all-to-all-done.1 = s32[32,1,1]{2,1,0:T(1,128)S(1)} async-done(((s32[32,1,1]{2,1,0:T(1,128)}), s32[32,1,1]{2,1,0:T(1,128)S(1)}, u32[]{:S(2)}, u32[]{:S(2)}) %all-to-all-start.1) | async-done | bytes 160 | tf_op jit(solution)/shard_map/all_to_all | solution.py:85
  37.4 3.9 %all-to-all-start.2 = ((bf16[32,1,2,2,128]{4,3,2,1,0:T(2,128)(2,1)}), bf16[32,1,2,2,128]{4,3,2,1,0:T(2,128)(2,1)S(1)}, u32[]{:S(2)}, u32[]{:S(2)}) async-start(bf16[32,1,2,2,128]{4,3,2,1,0:T(2,128)(2,1)} %bitcast.26), calls=%async_computation.2 | async-start | bytes 65536 | tf_op jit(solution)/shard_map/all_to_all | solution.py:83
  41.3 5.2 %broadcast_select_fusion = bf16[32,2,2,128,128]{4,3,2,1,0:T(8,128)(2,1)} fusion(bf16[32,2,2,128,128]{4,3,2,1,0:T(8,128)(2,1)} %bitcast.112, pred[32,2,128]{2,1,0:T(4,128)(4,1)S(1)} %get-tuple-element.16), kind=kLoop, calls=%fused_computation.8 | loop fusion | flops 2097152 | bytes 8396800 | tf_op jit(solution)/shard_map/jit(_where)/select_n | solution.py:76
  46.5 5.2 %gather_fusion.4 = bf16[32,2,2,128,128]{4,3,2,1,0:T(8,128)(2,1)} fusion(bf16[32,2,2,128,128]{4,3,2,1,0:T(8,128)(2,1)} %broadcast_select_fusion, s32[1024]{0:T(1024)S(1)} %pad_clamp_fusion), kind=kCustom, calls=%fused_computation.4 | custom fusion | bytes 8388736 | tf_op jit(solution)/shard_map/gather | solution.py:76
  51.7 0.0 all-to-all-done.2
  51.7 0.0 copy-start.6
  51.7 0.0 copy-start.5
  51.7 8.0 %all-to-all-start.3 = ((bf16[32,1,2,2,128,128]{5,4,3,2,1,0:T(8,128)(2,1)}), bf16[32,1,2,2,128,128]{5,4,3,2,1,0:T(8,128)(2,1)}, u32[]{:S(2)}, u32[]{:S(2)}) async-start(bf16[32,1,2,2,128,128]{5,4,3,2,1,0:T(8,128)(2,1)} %bitcast.114), calls=%async_computation.3 | async-start | bytes 8388608 | tf_op jit(solution)/shard_map/all_to_all | solution.py:87
  59.7 0.0 copy-done.6
  59.8 0.1 iota_compare_fusion.1
  59.9 0.0 copy-done.5
  59.9 0.1 fusion.32
  60.0 0.7 fusion.34
  60.7 2.7 %fusion.31 = (bf16[32,2,1,128,128]{4,3,2,1,0:T(8,128)(2,1)S(1)}, bf16[32,2,1,128,128]{4,3,2,1,0:T(8,128)(2,1)S(1)}) fusion(bf16[32,2,2,128,128]{4,3,2,1,0:T(8,128)(2,1)} %bitcast.113), kind=kLoop, calls=%fused_computation.76 | loop fusion | bytes 8388608 | tf_op jit(solution)/shard_map/slice | solution.py:89
  63.4 0.0 copy-start.2
  63.4 0.8 fusion.33
  64.2 0.1 fusion.22
  64.4 0.3 fusion.13
  64.7 0.3 convolution_bitcast_fusion
  64.9 0.0 copy-start.8
  64.9 0.5 fusion.4
  65.4 0.2 copy-done.2
  65.6 1.9 fusion.17
  67.5 0.0 copy-done.7
  67.5 0.7 compare_reduce_fusion
  68.2 0.1 iota_compare_fusion
  68.3 0.0 copy-done.8
  68.3 0.1 broadcast_select_fusion.2
  68.4 41.1 %all-to-all-done.3 = bf16[32,1,2,2,128,128]{5,4,3,2,1,0:T(8,128)(2,1)} async-done(((bf16[32,1,2,2,128,128]{5,4,3,2,1,0:T(8,128)(2,1)}), bf16[32,1,2,2,128,128]{5,4,3,2,1,0:T(8,128)(2,1)}, u32[]{:S(2)}, u32[]{:S(2)}) %all-to-all-start.3) | async-done | bytes 4194336 | tf_op jit(solution)/shard_map/all_to_all | solution.py:87
  109.5 5.6 %fusion.1 = bf16[32,2,2,128,128]{4,3,2,1,0:T(8,128)(2,1)S(1)} fusion(bf16[32,1,2,2,128,128]{5,4,3,2,1,0:T(8,128)(2,1)} %all-to-all-done.3, pred[32,2,128]{2,1,0:T(4,128)(4,1)S(1)} %get-tuple-element.14, pred[32,2,128]{2,1,0:T(4,128)(4,1)S(1)} %get-tuple-element.15, pred[32,2,128]{2,1,0:T(4,128)(4,1)S(1)} %get-tuple-element.13, ...), kind=kLoop, calls=%fused_computation.7 | loop fusion | flops 6291456 | bytes 8462336 | tf_op jit(solution)/shard_map/jit(_where)/select_n | solution.py:109
  115.1 0.0 copy-start.4
  115.1 0.6 fusion.30
  115.7 1.4 copy-done.4
  117.1 0.7 fusion.35
  117.9 0.2 fusion.16
  118.1 0.4 fusion.11
  118.5 0.8 copy-done.3
  119.3 1.6 fusion.23
  120.9 69.8 %all-reduce.2 = (bf16[64,4096]{1,0:T(8,128)(2,1)}, bf16[32,4096]{1,0:T(8,128)(2,1)}) all-reduce(f32[64,4096]{1,0:T(8,128)} %fusion.17, f32[32,4096]{1,0:T(8,128)} %fusion.23), channel_id=1, replica_groups=mesh['inst'=32,'tp'=8] {'tp'}, use_global_device_ids=true, to_apply=%region_4.5 | all-reduce | flops 393216 | bytes 2359296 | tf_op jit(solution)/shard_map/psum | solution.py:119
  190.7 2.2 %reshape.272 = bf16[32,2,4096]{2,1,0:T(2,128)(2,1)} reshape(bf16[64,4096]{1,0:T(8,128)(2,1)} %get-tuple-element.3) | data formatting | bytes 1048576 | tf_op jit(solution)/shard_map/reshape | solution.py:121
  (13 shorter events, 0.2 us)
Async XLA Ops:
  0.6 18.9 %copy-start = (bf16[48,2,128,128]{3,2,1,0:T(8,128)(2,1)S(1)}, bf16[48,2,128,128]{3,2,1,0:T(8,128)(2,1)}, u32[]{:S(2)}) copy-start(bf16[48,2,128,128]{3,2,1,0:T(8,128)(2,1)} %param.10) | copy-start | bytes 9437188
  4.5 18.1 %all-to-all-start = ((s32[32,1,1]{2,1,0:T(1,128)}), s32[32,1,1]{2,1,0:T(1,128)S(1)}, u32[]{:S(2)}, u32[]{:S(2)}) async-start(s32[32,1,1]{2,1,0:T(1,128)} %copy.42), calls=%async_computation | async-start | bytes 32768 | tf_op jit(solution)/shard_map/all_to_all | solution.py:84
  19.5 11.5 %copy-start.1 = (s32[32]{0:T(128)S(1)}, s32[32]{0:T(128)}, u32[]{:S(2)}) copy-start(s32[32]{0:T(128)} %param.12) | copy-start | bytes 388
  22.6 14.8 %all-to-all-start.1 = ((s32[32,1,1]{2,1,0:T(1,128)}), s32[32,1,1]{2,1,0:T(1,128)S(1)}, u32[]{:S(2)}, u32[]{:S(2)}) async-start(s32[32,1,1]{2,1,0:T(1,128)} %copy.43), calls=%async_computation.1 | async-start | bytes 32768 | tf_op jit(solution)/shard_map/all_to_all | solution.py:85
  37.4 14.3 %all-to-all-start.2 = ((bf16[32,1,2,2,128]{4,3,2,1,0:T(2,128)(2,1)}), bf16[32,1,2,2,128]{4,3,2,1,0:T(2,128)(2,1)S(1)}, u32[]{:S(2)}, u32[]{:S(2)}) async-start(bf16[32,1,2,2,128]{4,3,2,1,0:T(2,128)(2,1)} %bitcast.26), calls=%async_computation.2 | async-start | bytes 65536 | tf_op jit(solution)/shard_map/all_to_all | solution.py:83
  51.7 8.0 %copy-start.6 = (bf16[32,2,512]{2,1,0:T(2,128)(2,1)S(1)}, bf16[32,2,512]{2,1,0:T(2,128)(2,1)}, u32[]{:S(2)}) copy-start(bf16[32,2,512]{2,1,0:T(2,128)(2,1)} %param.15) | copy-start | bytes 196612
  51.7 8.2 %copy-start.5 = (bf16[32,2,2,128]{3,2,1,0:T(2,128)(2,1)S(1)}, bf16[32,2,2,128]{3,2,1,0:T(2,128)(2,1)}, u32[]{:S(2)}) copy-start(bf16[32,2,2,128]{3,2,1,0:T(2,128)(2,1)} %param.16) | copy-start | bytes 98308
  51.7 57.8 %all-to-all-start.3 = ((bf16[32,1,2,2,128,128]{5,4,3,2,1,0:T(8,128)(2,1)}), bf16[32,1,2,2,128,128]{5,4,3,2,1,0:T(8,128)(2,1)}, u32[]{:S(2)}, u32[]{:S(2)}) async-start(bf16[32,1,2,2,128,128]{5,4,3,2,1,0:T(8,128)(2,1)} %bitcast.114), calls=%async_computation.3 | async-start | bytes 8388608 | tf_op jit(solution)/shard_map/all_to_all | solution.py:87
  63.4 2.2 %copy-start.2 = (bf16[512,4096]{1,0:T(8,128)(2,1)S(1)}, bf16[512,4096]{1,0:T(8,128)(2,1)}, u32[]{:S(2)}) copy-start(bf16[512,4096]{1,0:T(8,128)(2,1)} %param.19) | copy-start | bytes 12582916
  64.9 2.6 %copy-start.7 = (bf16[32,512]{1,0:T(8,128)(2,1)S(1)}, bf16[32,512]{1,0:T(8,128)(2,1)}, u32[]{:S(2)}) copy-start(bf16[32,512]{1,0:T(8,128)(2,1)} %param.17) | copy-start | bytes 98308
  64.9 3.4 %copy-start.8 = (bf16[32,2,128]{2,1,0:T(2,128)(2,1)S(1)}, bf16[32,2,128]{2,1,0:T(2,128)(2,1)}, u32[]{:S(2)}) copy-start(bf16[32,2,128]{2,1,0:T(2,128)(2,1)} %param.18) | copy-start | bytes 49156
  115.1 2.0 %copy-start.4 = (bf16[32,2,2,128,128]{4,3,2,1,0:T(8,128)(2,1)}, bf16[32,2,2,128,128]{4,3,2,1,0:T(8,128)(2,1)S(1)}, u32[]{:S(2)}) copy-start(bf16[32,2,2,128,128]{4,3,2,1,0:T(8,128)(2,1)S(1)} %fusion.1) | copy-start | bytes 12582916
  117.1 2.2 %copy-start.3 = (bf16[512,4096]{1,0:T(8,128)(2,1)S(1)}, bf16[512,4096]{1,0:T(8,128)(2,1)}, u32[]{:S(2)}) copy-start(bf16[512,4096]{1,0:T(8,128)(2,1)} %param.19) | copy-start | bytes 12582916
where the time goes:
time: 194 us; the launch traced here: 193 us
  blocking collectives  69.8 us (36%)
  waiting for transfers between devices  47.3 us (24%)
  starting transfers between devices  28.8 us (15%)
  local copies, waits for them, and re-layouts  21.9 us (11%)
  other arithmetic  17.3 us (9%)
  matrix products  6.9 us (4%)
    psum x1, blocking collectives, shards(): src_total = lax.psum(partial_src, 'tp').astype(jnp.bfloat16)  69.8 us
    all_to_all x1, waiting for transfers between devices, shards(): lax.all_to_all(outgoing, 'inst', split_axis=0, concat_axis=0, tiled=True)  41.1 us
    all_to_all x1, starting transfers between devices, shards(): lax.all_to_all(len_out, 'inst', split_axis=0, concat_axis=0, tiled=True)  9.22 us
    all_to_all x1, starting transfers between devices, shards(): lax.all_to_all(outgoing, 'inst', split_axis=0, concat_axis=0, tiled=True)  7.99 us
    all_to_all x1, starting transfers between devices, shards(): lax.all_to_all(flag_out, 'inst', split_axis=0, concat_axis=0, tiled=True)  7.73 us
    all_to_all x1, waiting for transfers between devices, shards(): lax.all_to_all(flag_out, 'inst', split_axis=0, concat_axis=0, tiled=True)  6.24 us
    select_n x1, other arithmetic, shards(): filled = jnp.where(offset == 2, own_rows[:, None, :, None, :], filled)  5.59 us
    select_n x1, other arithmetic, shards(): outgoing = jnp.where(held[:, :, None, :, None], view, zero_value)[inverse]  5.25 us
  transfers between devices with their start and end apart: 4, of which 2 were waited for; matrix products, arithmetic and copies ran while one was open for 15% of the time, Pallas kernels for 0%

commit v1 on v0

v1 whole, which is shorter than its diff:
```python
import functools
import math

import jax
import jax.numpy as jnp
from jax import lax
from jax.experimental import pallas as pl
from jax.experimental.pallas import tpu as pltpu
from jax.sharding import PartitionSpec as P

MESH = pl.DeviceIdType.MESH
BF16 = jnp.bfloat16
F32 = jnp.float32
NEG = -1e30
HEAD = 128
PAGE = 128
GROUPS = 4
MIX = 11


def xor(a, b, bits):
    total = 0
    for bit in range(bits):
        weight = 2**bit
        u, v = (a // weight) % 2, (b // weight) % 2
        total = total + (u + v - 2 * u * v) * weight
    return total


def order(k, n):
    if n != 32:
        return (k * MIX) % n
    late = k // 16
    spot = (k - 16 * late) % 8
    turn = (k - 16 * late) // 8
    hop0 = (k % 3 + 1) // 2
    hop1 = 1 - (spot % 3 + 1) // 2
    hop = (1 - late) * hop0 + late * hop1
    cross0 = k - k // 3 - 1
    cross1 = 10 + 3 * turn + spot // 3
    plane0 = k // 3
    plane1 = 6 + 5 * turn + spot - spot // 3 - 1
    count = hop * ((1 - late) * cross0 + late * cross1)
    count = count + (1 - hop) * ((1 - late) * plane0 + late * plane1)
    return ((count * MIX) % 16) * 2 + hop


def kernel(
    n,
    tp_size,
    lens,
    tgts,
    mig,
    table,
    qsrc,
    fresh,
    qdst,
    rdst,
    pool_hbm,
    w_hbm,
    s_full,
    cache_out,
    d_full,
    pool,
    w,
    send,
    arr,
    qs,
    qd,
    att_s,
    att_d,
    s_half,
    s_half_in,
    s_pair,
    s_rs,
    s_rs_in,
    d_half,
    d_half_in,
    d_pair,
    d_rs,
    d_rs_in,
    load_sem,
    send_sem,
    recv_sem,
    half_sem,
    rs_sem,
    ag_sem,
    fwd_sem,
):
    me = lax.axis_index("inst")
    tp = lax.axis_index("tp")
    core = tp % 2
    hi = tp // 2
    his = tp_size // 2
    mate = tp + 1 - 2 * core
    bits = n.bit_length() - 1
    scale = 1.0 / math.sqrt(HEAD)
    cols = w.shape[1] // tp_size

    def peer_hi(step):
        return ((hi + step) % his) * 2 + core

    def partner(k):
        return xor(me, order(k, n), bits)

    barrier = pltpu.get_barrier_semaphore()

    def greet(k, _):
        pl.semaphore_signal(
            barrier, inc=1, device_id=(xor(me, k, bits), tp), device_id_type=MESH
        )
        return 0

    lax.fori_loop(1, n, greet, 0)
    pl.semaphore_signal(barrier, inc=1, device_id=(me, mate), device_id_type=MESH)
    for step in range(1, his):
        pl.semaphore_signal(barrier, inc=1, device_id=(me, peer_hi(step)), device_id_type=MESH)

    load_pool = pltpu.make_async_copy(pool_hbm, pool, load_sem.at[0])
    load_w = pltpu.make_async_copy(w_hbm, w, load_sem.at[1])
    load_pool.start()
    load_w.start()

    row = lax.broadcasted_iota(jnp.int32, (PAGE, HEAD), 0).astype(F32).astype(BF16)
    last = row == jnp.asarray(PAGE - 1, BF16)
    zero = jnp.zeros((PAGE, HEAD), BF16)

    def splat(value):
        return jnp.full((1, HEAD), value, F32)

    def move(k):
        peer = partner(k)
        return pltpu.make_async_remote_copy(
            src_ref=send.at[peer],
            dst_ref=arr.at[me],
            send_sem=send_sem.at[k],
            recv_sem=recv_sem.at[k],
            device_id=(peer, tp),
            device_id_type=MESH,
        )

    def arrive(k):
        peer = partner(k)
        return pltpu.make_async_remote_copy(
            src_ref=send.at[peer],
            dst_ref=arr.at[peer],
            send_sem=send_sem.at[k],
            recv_sem=recv_sem.at[k],
            device_id=(peer, tp),
            device_id_type=MESH,
        )

    def pack(k, ref):
        slot = partner(k)
        request = jnp.int32(0)
        for j in range(n):
            request = jnp.where(tgts[j] == slot, j, request)
        length = lens[request].astype(F32)
        flag = mig[request].astype(F32)
        rows_new = fresh[request].astype(F32)
        for p in range(2):
            at = splat(length - p * PAGE).astype(BF16)
            next_at = splat(length - p * PAGE + 1.0).astype(BF16)
            keep = row < at
            first = row == at
            second = row == next_at
            for c in range(2):
                page = pool[table[p, request], c]
                new0 = rows_new[0, c : c + 1].astype(BF16)
                new1 = rows_new[1, c : c + 1].astype(BF16)
                block = jnp.where(keep, page, zero)
                block = jnp.where(first, new0, block)
                block = jnp.where(second, new1, block)
                if p == 1:
                    note = splat(length if c == 0 else flag).astype(BF16)
                    block = jnp.where(last, note, block)
                ref[slot, p, c] = block

    load_pool.wait()
    pl.semaphore_wait(barrier, n - 1 + his)

    def send_step(k, _):
        pack(k, send)
        move(k).start()
        return 0

    batch = min(4, n)
    ahead = min(4 * batch, n)
    lax.fori_loop(1, ahead, send_step, 0)
    pack(0, send)
    arr[me] = send[me]

    def pack_step(k, _):
        pack(k, send)
        return 0

    lax.fori_loop(ahead, n, pack_step, 0)

    q_wide = qsrc[...].astype(F32)
    for g in range(GROUPS):
        lanes = slice(g * HEAD, (g + 1) * HEAD)
        for t in range(2):
            qs[:, 2 * g + t, :] = q_wide[:, t, lanes]
        qd[:, g, :] = qdst[:, lanes].astype(F32)

    def dot_t(a, b):
        return lax.dot_general(a, b, (((1,), (1,)), ((), ())), preferred_element_type=F32)

    def dot(a, b):
        return jnp.dot(a, b, preferred_element_type=F32)

    def soft(s0, s1):
        top = jnp.maximum(
            jnp.max(s0, axis=1, keepdims=True), jnp.max(s1, axis=1, keepdims=True)
        )
        e0, e1 = jnp.exp(s0 - top), jnp.exp(s1 - top)
        total = jnp.sum(e0, axis=1, keepdims=True) + jnp.sum(e1, axis=1, keepdims=True)
        return (e0 / total).astype(BF16), (e1 / total).astype(BF16)

    wide = min(8, n)
    lane8 = lax.broadcasted_iota(jnp.int32, (8, HEAD), 1)
    step8 = lax.broadcasted_iota(jnp.int32, (8, HEAD), 0) % 2

    def src_step(b, _):
        parts0, parts1 = [], []
        for i in range(wide):
            request = b * wide + i
            slot = tgts[request]
            query = qs[request].astype(BF16)
            bound = lens[request] + 1 + step8
            s0 = dot_t(query, send[slot, 0, 0]) * scale
            s1 = dot_t(query, send[slot, 1, 0]) * scale
            parts0.append(jnp.where(lane8 < bound, s0, NEG))
            parts1.append(jnp.where(lane8 + PAGE < bound, s1, NEG))
        w0, w1 = soft(jnp.concatenate(parts0, axis=0), jnp.concatenate(parts1, axis=0))
        for i in range(wide):
            request = b * wide + i
            slot = tgts[request]
            rows = slice(8 * i, 8 * i + 8)
            value1 = jnp.where(last, zero, send[slot, 1, 1])
            mixed = dot(w0[rows], send[slot, 0, 1]) + dot(w1[rows], value1)
            for g in range(GROUPS):
                att_s[g, pl.ds(2 * request, 2), :] = mixed[2 * g : 2 * g + 2]
        return 0

    lax.fori_loop(0, n // wide, src_step, 0)

    def remote(src, dst, sems, index, target):
        return pltpu.make_async_remote_copy(
            src_ref=src,
            dst_ref=dst,
            send_sem=sems.at[2 * index],
            recv_sem=sems.at[2 * index + 1],
            device_id=(me, target),
            device_id_type=MESH,
        )

    def block_cols(index):
        return pl.ds(pl.multiple_of(index * cols, cols), cols)

    def tail(part, att, half, half_in, pair, rs, rs_in, full):
        a = jnp.concatenate([att[g].astype(BF16) for g in range(GROUPS)], axis=1)

        def part_full(index):
            where = block_cols(index)
            return full.at[(slice(None),) * (len(full.shape) - 1) + (where,)]

        swap = remote(half, half_in, half_sem, part, mate)
        scatter = [
            remote(rs.at[step], rs_in.at[step], rs_sem, part * his + step, peer_hi(step))
            for step in range(1, his)
        ]
        mine = part_full(tp)
        gather = [
            remote(mine, mine, ag_sem, part * his + step, peer_hi(step))
            for step in range(1, his)
        ]
        landed = [
            remote(
                mine,
                part_full(((hi + his - step) % his) * 2 + core),
                ag_sem,
                part * his + step,
                peer_hi(step),
            )
            for step in range(1, his)
        ]
        forward = []
        received = []
        for step in range(his):
            owner = ((hi + his - step) % his) * 2
            have, want = part_full(owner + core), part_full(owner + 1 - core)
            forward.append(remote(have, have, fwd_sem, part * his + step, mate))
            received.append(remote(have, want, fwd_sem, part * his + step, mate))

        def one():
            for step in range(his):
                z = (hi + step) % his
                half[step] = dot(a, w[:, block_cols(z * 2 + 1 - core)]).astype(BF16)
            swap.start()
            for step in range(his):
                z = (hi + step) % his
                pair[step] = dot(a, w[:, block_cols(z * 2 + core)])

        def two():
            swap.wait()
            for step in range(1, his):
                rs[step] = (pair[step] + half_in[step].astype(F32)).astype(BF16)
                scatter[step - 1].start()
            pair[0] = pair[0] + half_in[0].astype(F32)

        def three():
            for copy in scatter:
                copy.wait()
            total = pair[0]
            for step in range(1, his):
                total = total + rs_in[step].astype(F32)
            if len(full.shape) == 3:
                total = total.reshape(full.shape[:2] + (cols,))
            mine[...] = total.astype(BF16)
            for copy in gather:
                copy.start()
            forward[0].start()

        def four():
            for step in range(1, his):
                landed[step - 1].wait_recv()
                forward[step].start()
            for step in range(his):
                received[step].wait_recv()

        def five():
            for copy in gather:
                copy.wait_send()
            for copy in forward:
                copy.wait_send()

        return one, two, three, four, five

    load_w.wait()
    src_tail = tail(0, att_s, s_half, s_half_in, s_pair, s_rs, s_rs_in, s_full)
    src_tail[0]()

    lane4 = lax.broadcasted_iota(jnp.int32, (GROUPS, HEAD), 1).astype(F32)

    def dst_step(b, _):
        slots, parts0, parts1, values = [], [], [], []
        for i in range(batch):
            k = b * batch + i

            @pl.when(k > 0)
            def _():
                move(k).wait_send()

            @pl.when(k + ahead < n)
            def _():
                move(k + ahead).start()

        for i in range(batch):
            k = b * batch + i
            slot = partner(k)
            slots.append(slot)

            @pl.when(k > 0)
            def _():
                arrive(k).wait_recv()

            length = arr[slot, 1, 0][PAGE - 1 :].astype(F32)
            flag = arr[slot, 1, 1][PAGE - 1 :].astype(F32)
            moved = jnp.broadcast_to(flag, (PAGE, HEAD)).astype(BF16) == jnp.asarray(1.0, BF16)
            own = rdst[slot].astype(F32)
            kept = []
            for p in range(2):
                at = (length + (2.0 - p * PAGE)).astype(BF16)
                hit = row == at
                for c in range(2):
                    block = arr[slot, p, c]
                    if p == 1:
                        block = jnp.where(last, zero, block)
                    block = jnp.where(hit, own[c : c + 1].astype(BF16), block)
                    block = jnp.where(moved, block, zero)
                    cache_out[slot, p, c] = block
                    kept.append(block)
            query = qd[slot].astype(BF16)
            bound = length + 3.0
            s0 = dot_t(query, kept[0]) * scale
            s1 = dot_t(query, kept[2]) * scale
            parts0.append(jnp.where(lane4 < bound, s0, NEG))
            parts1.append(jnp.where(lane4 + float(PAGE) < bound, s1, NEG))
            values.append((kept[1], kept[3]))
        for i in range(batch):
            w0, w1 = soft(parts0[i], parts1[i])
            mixed = dot(w0, values[i][0]) + dot(w1, values[i][1])
            for g in range(GROUPS):
                att_d[g, pl.ds(slots[i], 1), :] = mixed[g : g + 1]
        return 0

    steps = n // batch
    marks = [0, steps // 4, 3 * steps // 4, steps]
    lax.fori_loop(marks[0], marks[1], dst_step, 0)
    src_tail[1]()
    lax.fori_loop(marks[1], marks[2], dst_step, 0)
    src_tail[2]()
    lax.fori_loop(marks[2], marks[3], dst_step, 0)

    dst_tail = tail(1, att_d, d_half, d_half_in, d_pair, d_rs, d_rs_in, d_full)
    dst_tail[0]()
    src_tail[3]()
    for stage in dst_tail[1:]:
        stage()
    src_tail[4]()


def place(*refs):
    sem = refs[-1]
    half = len(refs) // 2
    copies = [
        pltpu.make_async_copy(src, dst, sem.at[i])
        for i, (src, dst) in enumerate(zip(refs[:half], refs[half:-1]))
    ]
    for copy in copies:
        copy.start()
    for copy in copies:
        copy.wait()


def shards(
    pool,
    page_table,
    lengths,
    targets,
    migrating,
    queries_src,
    new_rows,
    queries_dst,
    rows_dst,
    w_out,
):
    n = lax.axis_size("inst")
    tp_size = lax.axis_size("tp")
    his = tp_size // 2
    requests = queries_src.shape[0]
    width = w_out.shape[1]
    cols = width // tp_size
    smem = pl.BlockSpec(memory_space=pltpu.SMEM)
    vmem = pl.BlockSpec(memory_space=pltpu.VMEM)
    hbm = pl.BlockSpec(memory_space=pl.ANY)
    cache = (requests, 2, 2, PAGE, HEAD)

    def sums(rows):
        return [
            pltpu.VMEM((his, rows, cols), BF16),
            pltpu.VMEM((his, rows, cols), BF16),
            pltpu.VMEM((his, rows, cols), F32),
            pltpu.VMEM((his, rows, cols), BF16),
            pltpu.VMEM((his, rows, cols), BF16),
        ]

    dma = pltpu.SemaphoreType.DMA
    in_hbm = functools.partial(pltpu.with_memory_space_constraint, memory_space=pltpu.HBM)
    results = pl.pallas_call(
        functools.partial(kernel, n, tp_size),
        out_shape=(
            pltpu.VMEM((requests, 2, width), BF16),
            pltpu.VMEM(cache, BF16),
            pltpu.VMEM((requests, width), BF16),
        ),
        in_specs=[smem] * 4 + [vmem] * 4 + [hbm] * 2,
        out_specs=(vmem, vmem, vmem),
        scratch_shapes=[
            pltpu.VMEM(pool.shape, BF16),
            pltpu.VMEM(w_out.shape, BF16),
            pltpu.VMEM(cache, BF16),
            pltpu.VMEM(cache, BF16),
            pltpu.VMEM((requests, 2 * GROUPS, HEAD), F32),
            pltpu.VMEM((requests, GROUPS, HEAD), F32),
            pltpu.VMEM((GROUPS, 2 * requests, HEAD), F32),
            pltpu.VMEM((GROUPS, requests, HEAD), F32),
        ]
        + sums(2 * requests)
        + sums(requests)
        + [
            dma((2,)),
            dma((n,)),
            dma((n,)),
            dma((4,)),
            dma((4 * his,)),
            dma((4 * his,)),
            dma((4 * his,)),
        ],
        compiler_params=pltpu.CompilerParams(
            collective_id=0, has_side_effects=True, vmem_limit_bytes=28 * 1024 * 1024
        ),
        name="migrate",
    )(
        *map(
            in_hbm,
            (
                lengths,
                targets,
                migrating,
                page_table.T,
                queries_src,
                new_rows,
                queries_dst,
                rows_dst,
                pool,
                w_out,
            ),
        )
    )
    return pl.pallas_call(
        place,
        out_shape=tuple(pltpu.HBM(x.shape, x.dtype) for x in results),
        in_specs=[vmem] * 3,
        out_specs=(hbm,) * 3,
        scratch_shapes=[dma((3,))],
        compiler_params=pltpu.CompilerParams(vmem_limit_bytes=8 * 1024 * 1024),
        name="place",
    )(*(pltpu.with_memory_space_constraint(x, pltpu.VMEM) for x in results))


def solution(mesh):
    return jax.shard_map(
        shards,
        mesh=mesh,
        in_specs=(
            P("inst", None, None, "tp"),
            P("inst", None),
            P("inst"),
            P("inst"),
            P("inst"),
            P("inst", None, "tp"),
            P("inst", None, None, "tp"),
            P("inst", "tp"),
            P("inst", None, "tp"),
            P("tp", None),
        ),
        out_specs=(P("inst", None, None), P("inst", None, None, None, "tp"), P("inst", None)),
        check_vma=False,
    )
```

time: 194 us -> 91.3 us (0.47)
  Pallas kernels: 0 us -> 90 us
  blocking collectives: 69.8 us -> 0 us
  waiting for transfers between devices: 47.3 us -> 0 us
  starting transfers between devices: 28.8 us -> 0 us
  local copies, waits for them, and re-layouts: 21.9 us -> 0 us
  other arithmetic: 17.3 us -> 0 us
  matrix products: 6.9 us -> 0 us
    pallas_call x0 -> x2, Pallas kernels: none -> 90 us  [the longest x1 87.7 us: shards(): pl.pallas_call(functools.partial(kernel, n, tp_size), out_shape=(pltpu.VM...]
    psum x1 -> x0, blocking collectives: 69.8 us -> none  [shards(): src_total = lax.psum(partial_src, 'tp').astype(jnp.bfloat16)]
    all_to_all x4 -> x0, waiting for transfers between devices: 47.3 us -> none  [the longest x1 41.1 us: shards(): lax.all_to_all(outgoing, 'inst', split_axis=0, concat_axis=0, tiled=True)]
    all_to_all x4 -> x0, starting transfers between devices: 28.8 us -> none  [the longest x1 9.22 us: shards(): lax.all_to_all(len_out, 'inst', split_axis=0, concat_axis=0, tiled=True)]
    select_n x6 -> x0, other arithmetic: 12.5 us -> none  [the longest x1 5.59 us: shards(): filled = jnp.where(offset == 2, own_rows[:, None, :, None, :], filled)]
    gather x5 -> x0, local copies, waits for them, and re-layouts: 12.2 us -> none  [the longest x1 5.2 us: shards(): outgoing = jnp.where(held[:, :, None, :, None], view, zero_value)[inverse]]
    dot_general x8 -> x0, matrix products: 6.9 us -> none  [the longest x3 2.2 us: attend(): jnp.einsum('bthge,bshe->bthgs', query_heads, block_keys, preferred_elemen...]
    slice x3 -> x0, local copies, waits for them, and re-layouts: 3.37 us -> none  [the longest x1 2.74 us: shards(): old_values = view[:, :, 1].reshape(requests, span, heads_local, head_size)]
  transfers between devices with their start and end apart: 4 -> 0, of which waited for: 2 -> 0; matrix products, arithmetic and copies ran while one was open for 15% -> 0% of each run, Pallas kernels for 0% -> 0%
where the time goes in v1:
time: 91.3 us; the launch traced here: 90.6 us
  Pallas kernels  90 us (99%)
    pallas_call x1, Pallas kernels, shards(): pl.pallas_call(functools.partial(kernel, n, tp_size), out_shape=(pltpu.VM...  87.7 us
    pallas_call x1, Pallas kernels, shards(): pl.pallas_call(place, out_shape=tuple((pltpu.HBM(x.shape, x.dtype) for x...  2.28 us

profile of v1, /device:TPU:1, one launch (start us, length us, event | category | flops | bytes accessed | tf_op | source)
XLA Modules:
  0.0 90.6 jit_solution(6560427138245269071)
XLA Ops:
  0.6 87.7 %migrate.1 = (bf16[32,2,4096]{2,1,0:T(2,128)(2,1)S(1)}, bf16[32,2,2,128,128]{4,3,2,1,0:T(8,128)(2,1)S(1)}, bf16[32,4096]{1,0:T(8,128)(2,1)S(1)}) custom-call(s32[32]{0:T(128)} %lens.1, s32[32]{0:T(128)} %tgts.1, s32[32]{0:T(128)} %mig.1, s32[2,32]{1,0:T(2,128)} %bitcast.1, bf16[32,2,512]{2,1,0:T(2,128)(2,1)} %qsrc.1, bf16[32,2,2,128]{3,2,1,0:T(2,128)(2,1)} %fresh.1, ...), custom_call_target="tpu_custom_call" | custom-call | tf_op jit(solution)/shard_map/migrate/pallas_call | solution.py:461
  88.3 2.3 %place.1 = (bf16[32,2,4096]{2,1,0:T(2,128)(2,1)}, bf16[32,2,2,128,128]{4,3,2,1,0:T(8,128)(2,1)}, bf16[32,4096]{1,0:T(8,128)(2,1)}) custom-call(bf16[32,2,4096]{2,1,0:T(2,128)(2,1)S(1)} %get-tuple-element.6.refs_0_, bf16[32,2,2,128,128]{4,3,2,1,0:T(8,128)(2,1)S(1)} %get-tuple-element.7.refs_1_, bf16[32,4096]{1,0:T(8,128)(2,1)S(1)} %get-tuple-element.8.refs_2_), custom_call_target="tpu_custom_call" | custom-call | tf_op jit(solution)/shard_map/place/pallas_call | solution.py:512

commit v2 on v1

--- a/solution.py
+++ b/solution.py
@@ -72,6 +72,8 @@
     s_half,
     s_half_in,
     s_pair,
+    s_cross,
+    s_cross_in,
     s_rs,
     s_rs_in,
     d_half,
@@ -103,6 +105,9 @@
     def partner(k):
         return xor(me, order(k, n), bits)
 
+    load_pool = pltpu.make_async_copy(pool_hbm, pool, load_sem.at[0])
+    load_w = pltpu.make_async_copy(w_hbm, w, load_sem.at[1])
+    load_pool.start()
     barrier = pltpu.get_barrier_semaphore()
 
     def greet(k, _):
@@ -115,11 +120,6 @@
     pl.semaphore_signal(barrier, inc=1, device_id=(me, mate), device_id_type=MESH)
     for step in range(1, his):
         pl.semaphore_signal(barrier, inc=1, device_id=(me, peer_hi(step)), device_id_type=MESH)
-
-    load_pool = pltpu.make_async_copy(pool_hbm, pool, load_sem.at[0])
-    load_w = pltpu.make_async_copy(w_hbm, w, load_sem.at[1])
-    load_pool.start()
-    load_w.start()
 
     row = lax.broadcasted_iota(jnp.int32, (PAGE, HEAD), 0).astype(F32).astype(BF16)
     last = row == jnp.asarray(PAGE - 1, BF16)
@@ -176,32 +176,26 @@
                     block = jnp.where(last, note, block)
                 ref[slot, p, c] = block
 
-    load_pool.wait()
-    pl.semaphore_wait(barrier, n - 1 + his)
-
-    def send_step(k, _):
-        pack(k, send)
-        move(k).start()
-        return 0
-
-    batch = min(4, n)
-    ahead = min(4 * batch, n)
-    lax.fori_loop(1, ahead, send_step, 0)
-    pack(0, send)
-    arr[me] = send[me]
-
-    def pack_step(k, _):
-        pack(k, send)
-        return 0
-
-    lax.fori_loop(ahead, n, pack_step, 0)
-
     q_wide = qsrc[...].astype(F32)
     for g in range(GROUPS):
         lanes = slice(g * HEAD, (g + 1) * HEAD)
         for t in range(2):
             qs[:, 2 * g + t, :] = q_wide[:, t, lanes]
         qd[:, g, :] = qdst[:, lanes].astype(F32)
+
+    load_pool.wait()
+    pl.semaphore_wait(barrier, n - 1 + his)
+    load_w.start()
+
+    def send_step(k, _):
+        pack(k, send)
+        move(k).start()
+        return 0
+
+    batch = min(4, n)
+    lax.fori_loop(1, n, send_step, 0)
+    pack(0, send)
+    arr[me] = send[me]
 
     def dot_t(a, b):
         return lax.dot_general(a, b, (((1,), (1,)), ((), ())), preferred_element_type=F32)
@@ -258,12 +252,106 @@
     def block_cols(index):
         return pl.ds(pl.multiple_of(index * cols, cols), cols)
 
+    def ring_tail(att, half, half_in, pair, cross, cross_in, rs, rs_in, full):
+        a = jnp.concatenate([att[g].astype(BF16) for g in range(GROUPS)], axis=1)
+        part = cols // 2
+        up, down = peer_hi(1), peer_hi(his - 1)
+
+        def spot(step, side=None):
+            start = (((hi + step) % his) * 2 + core) * cols
+            if side is None:
+                return full.at[:, :, pl.ds(pl.multiple_of(start, cols), cols)]
+            return full.at[:, :, pl.ds(pl.multiple_of(start + side * part, part), part)]
+
+        def mates(step):
+            start = (((hi + step) % his) * 2 + 1 - core) * cols
+            return full.at[:, :, pl.ds(pl.multiple_of(start, cols), cols)]
+
+        swap = remote(half, half_in, half_sem, 0, mate)
+        over = [
+            remote(cross.at[0], cross_in.at[0], rs_sem, 0, up),
+            remote(cross.at[1], cross_in.at[1], rs_sem, 1, down),
+        ]
+        near = [
+            remote(rs.at[0], rs_in.at[0], rs_sem, 2, up),
+            remote(rs.at[1], rs_in.at[1], rs_sem, 3, down),
+        ]
+        give = [remote(spot(0), spot(0), ag_sem, i, to) for i, to in enumerate((up, down))]
+        take = [
+            remote(spot(0), spot(step), ag_sem, i, to)
+            for i, (step, to) in enumerate(((his - 1, up), (1, down)))
+        ]
+        pass_on = [
+            remote(spot(step, side), spot(step, side), ag_sem, 2 + side, to)
+            for side, (step, to) in enumerate(((his - 1, up), (1, down)))
+        ]
+        last_in = [
+            remote(spot(0, side), spot(2, side), ag_sem, 2 + side, to)
+            for side, to in enumerate((up, down))
+        ]
+        forward = [remote(spot(step), spot(step), fwd_sem, step, mate) for step in range(his)]
+        received = [remote(spot(step), mates(step), fwd_sem, step, mate) for step in range(his)]
+
+        def project():
+            for step in range(his):
+                z = (hi + step) % his
+                half[step] = dot(a, w[:, block_cols(z * 2 + 1 - core)]).astype(BF16)
+            swap.start()
+            for step in range(his):
+                z = (hi + step) % his
+                pair[step] = dot(a, w[:, block_cols(z * 2 + core)])
+
+        def far():
+            swap.wait()
+            for step in range(his):
+                pair[step] = pair[step] + half_in[step].astype(F32)
+            cross[0] = pair[2, :, :part].astype(BF16)
+            cross[1] = pair[2, :, part:].astype(BF16)
+            for copy in over:
+                copy.start()
+
+        def close():
+            for copy in over:
+                copy.wait()
+            rs[0, :, :part] = (pair[1, :, :part] + cross_in[0].astype(F32)).astype(BF16)
+            rs[0, :, part:] = pair[1, :, part:].astype(BF16)
+            rs[1, :, :part] = pair[his - 1, :, :part].astype(BF16)
+            rs[1, :, part:] = (pair[his - 1, :, part:] + cross_in[1].astype(F32)).astype(BF16)
+            for copy in near:
+                copy.start()
+
+        def total():
+            for copy in near:
+                copy.wait()
+            sums = pair[0] + rs_in[0].astype(F32) + rs_in[1].astype(F32)
+            spot(0)[...] = sums.reshape(full.shape[:2] + (cols,)).astype(BF16)
+            for copy in give:
+                copy.start()
+            forward[0].start()
+
+        def relay():
+            for side, step in enumerate((his - 1, 1)):
+                take[side].wait_recv()
+                pass_on[side].start()
+                forward[step].start()
+
+        def end():
+            for copy in last_in:
+                copy.wait_recv()
+            forward[2].start()
+            for copy in received:
+                copy.wait_recv()
+            for copy in give + pass_on + forward:
+                copy.wait_send()
+
+        return project, far, close, total, relay, end
+
     def tail(part, att, half, half_in, pair, rs, rs_in, full):
         a = jnp.concatenate([att[g].astype(BF16) for g in range(GROUPS)], axis=1)
 
         def part_full(index):
             where = block_cols(index)
-            return full.at[(slice(None),) * (len(full.shape) - 1) + (where,)]
+            return full.at[:, where]
 
         swap = remote(half, half_in, half_sem, part, mate)
         scatter = [
@@ -315,8 +403,6 @@
             total = pair[0]
             for step in range(1, his):
                 total = total + rs_in[step].astype(F32)
-            if len(full.shape) == 3:
-                total = total.reshape(full.shape[:2] + (cols,))
             mine[...] = total.astype(BF16)
             for copy in gather:
                 copy.start()
@@ -338,8 +424,10 @@
         return one, two, three, four, five
 
     load_w.wait()
-    src_tail = tail(0, att_s, s_half, s_half_in, s_pair, s_rs, s_rs_in, s_full)
-    src_tail[0]()
+    project, far, close, total_up, relay, end = ring_tail(
+        att_s, s_half, s_half_in, s_pair, s_cross, s_cross_in, s_rs, s_rs_in, s_full
+    )
+    project()
 
     lane4 = lax.broadcasted_iota(jnp.int32, (GROUPS, HEAD), 1).astype(F32)
 
@@ -351,10 +439,6 @@
             @pl.when(k > 0)
             def _():
                 move(k).wait_send()
-
-            @pl.when(k + ahead < n)
-            def _():
-                move(k + ahead).start()
 
         for i in range(batch):
             k = b * batch + i
@@ -396,19 +480,21 @@
         return 0
 
     steps = n // batch
-    marks = [0, steps // 4, 3 * steps // 4, steps]
+    marks = [steps * j // 8 for j in (0, 2, 4, 6, 8)]
     lax.fori_loop(marks[0], marks[1], dst_step, 0)
-    src_tail[1]()
+    far()
     lax.fori_loop(marks[1], marks[2], dst_step, 0)
-    src_tail[2]()
+    close()
     lax.fori_loop(marks[2], marks[3], dst_step, 0)
+    total_up()
+    lax.fori_loop(marks[3], marks[4], dst_step, 0)
 
     dst_tail = tail(1, att_d, d_half, d_half_in, d_pair, d_rs, d_rs_in, d_full)
     dst_tail[0]()
-    src_tail[3]()
+    relay()
     for stage in dst_tail[1:]:
         stage()
-    src_tail[4]()
+    end()
 
 
 def place(*refs):
@@ -447,14 +533,12 @@
     hbm = pl.BlockSpec(memory_space=pl.ANY)
     cache = (requests, 2, 2, PAGE, HEAD)
 
-    def sums(rows):
+    def sums(rows, sent):
         return [
             pltpu.VMEM((his, rows, cols), BF16),
             pltpu.VMEM((his, rows, cols), BF16),
             pltpu.VMEM((his, rows, cols), F32),
-            pltpu.VMEM((his, rows, cols), BF16),
-            pltpu.VMEM((his, rows, cols), BF16),
-        ]
+        ] + [pltpu.VMEM((parts, rows, width), BF16) for parts, width in sent]
 
     dma = pltpu.SemaphoreType.DMA
     in_hbm = functools.partial(pltpu.with_memory_space_constraint, memory_space=pltpu.HBM)
@@ -477,8 +561,8 @@
             pltpu.VMEM((GROUPS, 2 * requests, HEAD), F32),
             pltpu.VMEM((GROUPS, requests, HEAD), F32),
         ]
-        + sums(2 * requests)
-        + sums(requests)
+        + sums(2 * requests, [(2, cols // 2)] * 2 + [(2, cols)] * 2)
+        + sums(requests, [(his, cols)] * 2)
         + [
             dma((2,)),
             dma((n,)),

time: 91.3 us -> 93.2 us (1.021)
  Pallas kernels: 90 us -> 91.1 us
    pallas_call x1, Pallas kernels: 87.7 us -> 88.8 us  [shards(): pl.pallas_call(functools.partial(kernel, n, tp_size), out_shape=(pltpu.VM...]
where the time goes in v2:
time: 93.2 us; the launch traced here: 91.7 us
  Pallas kernels  91.1 us (98%)
    pallas_call x1, Pallas kernels, shards(): pl.pallas_call(functools.partial(kernel, n, tp_size), out_shape=(pltpu.VM...  88.8 us
    pallas_call x1, Pallas kernels, shards(): pl.pallas_call(place, out_shape=tuple((pltpu.HBM(x.shape, x.dtype) for x...  2.28 us

profile of v2, /device:TPU:1, one launch (start us, length us, event | category | flops | bytes accessed | tf_op | source)
XLA Modules:
  0.0 91.7 jit_solution(18115433676324798997)
XLA Ops:
  0.6 88.8 %migrate.1 = (bf16[32,2,4096]{2,1,0:T(2,128)(2,1)S(1)}, bf16[32,2,2,128,128]{4,3,2,1,0:T(8,128)(2,1)S(1)}, bf16[32,4096]{1,0:T(8,128)(2,1)S(1)}) custom-call(s32[32]{0:T(128)} %lens.1, s32[32]{0:T(128)} %tgts.1, s32[32]{0:T(128)} %mig.1, s32[2,32]{1,0:T(2,128)} %bitcast.1, bf16[32,2,512]{2,1,0:T(2,128)(2,1)} %qsrc.1, bf16[32,2,2,128]{3,2,1,0:T(2,128)(2,1)} %fresh.1, ...), custom_call_target="tpu_custom_call" | custom-call | tf_op jit(solution)/shard_map/migrate/pallas_call | solution.py:545
  89.4 2.3 %place.1 = (bf16[32,2,4096]{2,1,0:T(2,128)(2,1)}, bf16[32,2,2,128,128]{4,3,2,1,0:T(8,128)(2,1)}, bf16[32,4096]{1,0:T(8,128)(2,1)}) custom-call(bf16[32,2,4096]{2,1,0:T(2,128)(2,1)S(1)} %get-tuple-element.6.refs_0_, bf16[32,2,2,128,128]{4,3,2,1,0:T(8,128)(2,1)S(1)} %get-tuple-element.7.refs_1_, bf16[32,4096]{1,0:T(8,128)(2,1)S(1)} %get-tuple-element.8.refs_2_), custom_call_target="tpu_custom_call" | custom-call | tf_op jit(solution)/shard_map/place/pallas_call | solution.py:596

commit v3 on v1

--- a/solution.py
+++ b/solution.py
@@ -15,34 +15,17 @@
 HEAD = 128
 PAGE = 128
 GROUPS = 4
-MIX = 11
-
-
-def xor(a, b, bits):
-    total = 0
-    for bit in range(bits):
-        weight = 2**bit
-        u, v = (a // weight) % 2, (b // weight) % 2
-        total = total + (u + v - 2 * u * v) * weight
-    return total
-
-
-def order(k, n):
+MIX = 19
+FIRST = 13
+TURN = 5
+
+
+def shift(a, b, n, sign):
     if n != 32:
-        return (k * MIX) % n
-    late = k // 16
-    spot = (k - 16 * late) % 8
-    turn = (k - 16 * late) // 8
-    hop0 = (k % 3 + 1) // 2
-    hop1 = 1 - (spot % 3 + 1) // 2
-    hop = (1 - late) * hop0 + late * hop1
-    cross0 = k - k // 3 - 1
-    cross1 = 10 + 3 * turn + spot // 3
-    plane0 = k // 3
-    plane1 = 6 + 5 * turn + spot - spot // 3 - 1
-    count = hop * ((1 - late) * cross0 + late * cross1)
-    count = count + (1 - hop) * ((1 - late) * plane0 + late * plane1)
-    return ((count * MIX) % 16) * 2 + hop
+        return (a + n + sign * b) % n
+    y = (a // 8 + 4 + sign * (b // 8)) % 4
+    x = ((a // 2) % 4 + 4 + sign * ((b // 2) % 4)) % 4
+    return y * 8 + x * 2 + (a + b) % 2
 
 
 def kernel(
@@ -60,7 +43,7 @@
     w_hbm,
     s_full,
     cache_out,
-    d_full,
+    d_out,
     pool,
     w,
     send,
@@ -74,11 +57,17 @@
     s_pair,
     s_rs,
     s_rs_in,
+    e_half,
+    e_half_in,
+    e_pair,
+    e_rs,
+    e_rs_in,
     d_half,
     d_half_in,
     d_pair,
     d_rs,
     d_rs_in,
+    d_rows,
     load_sem,
     send_sem,
     recv_sem,
@@ -93,21 +82,36 @@
     hi = tp // 2
     his = tp_size // 2
     mate = tp + 1 - 2 * core
-    bits = n.bit_length() - 1
     scale = 1.0 / math.sqrt(HEAD)
     cols = w.shape[1] // tp_size
 
     def peer_hi(step):
         return ((hi + step) % his) * 2 + core
 
-    def partner(k):
-        return xor(me, order(k, n), bits)
-
+    def item(k):
+        half = n // 2
+        return (k // half) * half + (k % half + TURN * core) % half
+
+    def offset_of(index):
+        return (index * MIX + FIRST) % n
+
+    def offset(k):
+        return offset_of(item(k))
+
+    def target(k):
+        return shift(me, offset(k), n, 1)
+
+    def origin(k):
+        return shift(me, offset(k), n, -1)
+
+    load_pool = pltpu.make_async_copy(pool_hbm, pool, load_sem.at[0])
+    load_w = pltpu.make_async_copy(w_hbm, w, load_sem.at[1])
+    load_pool.start()
     barrier = pltpu.get_barrier_semaphore()
 
     def greet(k, _):
         pl.semaphore_signal(
-            barrier, inc=1, device_id=(xor(me, k, bits), tp), device_id_type=MESH
+            barrier, inc=1, device_id=((me + k) % n, tp), device_id_type=MESH
         )
         return 0
 
@@ -116,11 +120,6 @@
     for step in range(1, his):
         pl.semaphore_signal(barrier, inc=1, device_id=(me, peer_hi(step)), device_id_type=MESH)
 
-    load_pool = pltpu.make_async_copy(pool_hbm, pool, load_sem.at[0])
-    load_w = pltpu.make_async_copy(w_hbm, w, load_sem.at[1])
-    load_pool.start()
-    load_w.start()
-
     row = lax.broadcasted_iota(jnp.int32, (PAGE, HEAD), 0).astype(F32).astype(BF16)
     last = row == jnp.asarray(PAGE - 1, BF16)
     zero = jnp.zeros((PAGE, HEAD), BF16)
@@ -129,7 +128,7 @@
         return jnp.full((1, HEAD), value, F32)
 
     def move(k):
-        peer = partner(k)
+        peer = target(k)
         return pltpu.make_async_remote_copy(
             src_ref=send.at[peer],
             dst_ref=arr.at[me],
@@ -140,7 +139,7 @@
         )
 
     def arrive(k):
-        peer = partner(k)
+        peer = origin(k)
         return pltpu.make_async_remote_copy(
             src_ref=send.at[peer],
             dst_ref=arr.at[peer],
@@ -151,7 +150,7 @@
         )
 
     def pack(k, ref):
-        slot = partner(k)
+        slot = target(k)
         request = jnp.int32(0)
         for j in range(n):
             request = jnp.where(tgts[j] == slot, j, request)
@@ -176,32 +175,50 @@
                     block = jnp.where(last, note, block)
                 ref[slot, p, c] = block
 
-    load_pool.wait()
-    pl.semaphore_wait(barrier, n - 1 + his)
-
-    def send_step(k, _):
-        pack(k, send)
-        move(k).start()
-        return 0
-
-    batch = min(4, n)
-    ahead = min(4 * batch, n)
-    lax.fori_loop(1, ahead, send_step, 0)
-    pack(0, send)
-    arr[me] = send[me]
-
-    def pack_step(k, _):
-        pack(k, send)
-        return 0
-
-    lax.fori_loop(ahead, n, pack_step, 0)
-
     q_wide = qsrc[...].astype(F32)
     for g in range(GROUPS):
         lanes = slice(g * HEAD, (g + 1) * HEAD)
         for t in range(2):
             qs[:, 2 * g + t, :] = q_wide[:, t, lanes]
         qd[:, g, :] = qdst[:, lanes].astype(F32)
+
+    load_pool.wait()
+    pl.semaphore_wait(barrier, n - 1 + his)
+    load_w.start()
+
+    def go(k):
+        @pl.when(offset(k) != 0)
+        def _():
+            move(k).start()
+
+    def send_step(k, _):
+        pack(k, send)
+        go(k)
+        return 0
+
+    batch = min(4, n)
+    ahead = min(8, n // 2)
+
+    def tick(j):
+        @pl.when(offset(j) != 0)
+        def _():
+            move(j).wait_send()
+
+        go(j + ahead)
+
+    lax.fori_loop(0, ahead, send_step, 0)
+
+    def pack_step(k, _):
+        pack(k, send)
+
+        @pl.when(k % 4 == 3)
+        def _():
+            tick((k - ahead) // 4)
+
+        return 0
+
+    lax.fori_loop(ahead, n, pack_step, 0)
+    arr[me] = send[me]
 
     def dot_t(a, b):
         return lax.dot_general(a, b, (((1,), (1,)), ((), ())), preferred_element_type=F32)
@@ -223,6 +240,7 @@
 
     def src_step(b, _):
         parts0, parts1 = [], []
+        tick((n - ahead) // 4 + b)
         for i in range(wide):
             request = b * wide + i
             slot = tgts[request]
@@ -258,12 +276,14 @@
     def block_cols(index):
         return pl.ds(pl.multiple_of(index * cols, cols), cols)
 
-    def tail(part, att, half, half_in, pair, rs, rs_in, full):
-        a = jnp.concatenate([att[g].astype(BF16) for g in range(GROUPS)], axis=1)
+    def tail(part, att, rows, half, half_in, pair, rs, rs_in, full):
+        a = jnp.concatenate([att[g, rows].astype(BF16) for g in range(GROUPS)], axis=1)
 
         def part_full(index):
             where = block_cols(index)
-            return full.at[(slice(None),) * (len(full.shape) - 1) + (where,)]
+            if len(full.shape) == 2:
+                return full.at[rows, where]
+            return full.at[:, :, where]
 
         swap = remote(half, half_in, half_sem, part, mate)
         scatter = [
@@ -337,34 +357,33 @@
 
         return one, two, three, four, five
 
+    ticked = (n - ahead) // 4 + n // wide
     load_w.wait()
-    src_tail = tail(0, att_s, s_half, s_half_in, s_pair, s_rs, s_rs_in, s_full)
+    src_tail = tail(0, att_s, slice(None), s_half, s_half_in, s_pair, s_rs, s_rs_in, s_full)
     src_tail[0]()
 
     lane4 = lax.broadcasted_iota(jnp.int32, (GROUPS, HEAD), 1).astype(F32)
 
     def dst_step(b, _):
         slots, parts0, parts1, values = [], [], [], []
+        for i in range(2):
+            j = ticked + 2 * b + i
+
+            @pl.when(j + ahead < n)
+            def _():
+                tick(j)
+
         for i in range(batch):
             k = b * batch + i
 
-            @pl.when(k > 0)
+            @pl.when(offset(k) != 0)
             def _():
-                move(k).wait_send()
-
-            @pl.when(k + ahead < n)
-            def _():
-                move(k + ahead).start()
+                arrive(k).wait_recv()
 
         for i in range(batch):
             k = b * batch + i
-            slot = partner(k)
+            slot = origin(k)
             slots.append(slot)
-
-            @pl.when(k > 0)
-            def _():
-                arrive(k).wait_recv()
-
             length = arr[slot, 1, 0][PAGE - 1 :].astype(F32)
             flag = arr[slot, 1, 1][PAGE - 1 :].astype(F32)
             moved = jnp.broadcast_to(flag, (PAGE, HEAD)).astype(BF16) == jnp.asarray(1.0, BF16)
@@ -392,23 +411,51 @@
             w0, w1 = soft(parts0[i], parts1[i])
             mixed = dot(w0, values[i][0]) + dot(w1, values[i][1])
             for g in range(GROUPS):
-                att_d[g, pl.ds(slots[i], 1), :] = mixed[g : g + 1]
+                att_d[g, pl.ds(item(b * batch + i), 1), :] = mixed[g : g + 1]
         return 0
 
     steps = n // batch
-    marks = [0, steps // 4, 3 * steps // 4, steps]
+    marks = [steps * j // 8 for j in (0, 1, 3, 4, 6, 8)]
     lax.fori_loop(marks[0], marks[1], dst_step, 0)
     src_tail[1]()
     lax.fori_loop(marks[1], marks[2], dst_step, 0)
     src_tail[2]()
     lax.fori_loop(marks[2], marks[3], dst_step, 0)
-
-    dst_tail = tail(1, att_d, d_half, d_half_in, d_pair, d_rs, d_rs_in, d_full)
-    dst_tail[0]()
+    early = tail(1, att_d, slice(0, n // 2), e_half, e_half_in, e_pair, e_rs, e_rs_in, d_rows)
+    early[0]()
+    early[1]()
+    lax.fori_loop(marks[3], marks[4], dst_step, 0)
     src_tail[3]()
-    for stage in dst_tail[1:]:
+    early[2]()
+    lax.fori_loop(marks[4], marks[5], dst_step, 0)
+
+    late = tail(2, att_d, slice(n // 2, n), d_half, d_half_in, d_pair, d_rs, d_rs_in, d_rows)
+    late[0]()
+    early[3]()
+    for stage in late[1:4]:
         stage()
+
+    lane = lax.broadcasted_iota(jnp.int32, (n, HEAD), 1)
+    owner = jnp.full((n, HEAD), -1, jnp.int32)
+    for k in range(n):
+        owner = jnp.where(lane == k, shift(me, offset_of(k), n, -1), owner)
+    place_row = lax.broadcasted_iota(jnp.int32, (n, HEAD), 0) == owner
+    spread = jnp.where(place_row, 1.0, 0.0).astype(BF16)[:, :n]
+    for index in range(tp_size):
+        where = slice(index * cols, (index + 1) * cols)
+        d_out[:, where] = dot(spread, d_rows[:, where]).astype(BF16)
+
+    def drain(k, _):
+        @pl.when(offset(k) != 0)
+        def _():
+            move(k).wait_send()
+
+        return 0
+
+    lax.fori_loop(n - ahead, n, drain, 0)
     src_tail[4]()
+    early[4]()
+    late[4]()
 
 
 def place(*refs):
@@ -478,15 +525,17 @@
             pltpu.VMEM((GROUPS, requests, HEAD), F32),
         ]
         + sums(2 * requests)
-        + sums(requests)
+        + sums(requests // 2)
+        + sums(requests // 2)
+        + [pltpu.VMEM((requests, width), BF16)]
         + [
             dma((2,)),
             dma((n,)),
             dma((n,)),
-            dma((4,)),
-            dma((4 * his,)),
-            dma((4 * his,)),
-            dma((4 * his,)),
+            dma((6,)),
+            dma((6 * his,)),
+            dma((6 * his,)),
+            dma((6 * his,)),
         ],
         compiler_params=pltpu.CompilerParams(
             collective_id=0, has_side_effects=True, vmem_limit_bytes=28 * 1024 * 1024

time: 91.3 us -> 94.4 us (1.034)
  Pallas kernels: 90 us -> 92.9 us
    pallas_call x1, Pallas kernels: 87.7 us -> 90.6 us  [shards(): pl.pallas_call(functools.partial(kernel, n, tp_size), out_shape=(pltpu.VM...]
where the time goes in v3:
time: 94.4 us; the launch traced here: 93.5 us
  Pallas kernels  92.9 us (98%)
    pallas_call x1, Pallas kernels, shards(): pl.pallas_call(functools.partial(kernel, n, tp_size), out_shape=(pltpu.VM...  90.6 us
    pallas_call x1, Pallas kernels, shards(): pl.pallas_call(place, out_shape=tuple((pltpu.HBM(x.shape, x.dtype) for x...  2.28 us

profile of v3, /device:TPU:1, one launch (start us, length us, event | category | flops | bytes accessed | tf_op | source)
XLA Modules:
  0.0 93.5 jit_solution(2243804594402477061)
XLA Ops:
  0.6 90.6 %migrate.1 = (bf16[32,2,4096]{2,1,0:T(2,128)(2,1)S(1)}, bf16[32,2,2,128,128]{4,3,2,1,0:T(8,128)(2,1)S(1)}, bf16[32,4096]{1,0:T(8,128)(2,1)S(1)}) custom-call(s32[32]{0:T(128)} %lens.1, s32[32]{0:T(128)} %tgts.1, s32[32]{0:T(128)} %mig.1, s32[2,32]{1,0:T(2,128)} %bitcast.1, bf16[32,2,512]{2,1,0:T(2,128)(2,1)} %qsrc.1, bf16[32,2,2,128]{3,2,1,0:T(2,128)(2,1)} %fresh.1, ...), custom_call_target="tpu_custom_call" | custom-call | tf_op jit(solution)/shard_map/migrate/pallas_call | solution.py:508
  91.2 2.3 %place.1 = (bf16[32,2,4096]{2,1,0:T(2,128)(2,1)}, bf16[32,2,2,128,128]{4,3,2,1,0:T(8,128)(2,1)}, bf16[32,4096]{1,0:T(8,128)(2,1)}) custom-call(bf16[32,2,4096]{2,1,0:T(2,128)(2,1)S(1)} %get-tuple-element.6.refs_0_, bf16[32,2,2,128,128]{4,3,2,1,0:T(8,128)(2,1)S(1)} %get-tuple-element.7.refs_1_, bf16[32,4096]{1,0:T(8,128)(2,1)S(1)} %get-tuple-element.8.refs_2_), custom_call_target="tpu_custom_call" | custom-call | tf_op jit(solution)/shard_map/place/pallas_call | solution.py:561

commit v4 on v2

--- a/solution.py
+++ b/solution.py
@@ -15,6 +15,8 @@
 HEAD = 128
 PAGE = 128
 GROUPS = 4
+TILE = 16
+PIECES = 8
 MIX = 11
 
 
@@ -124,9 +126,7 @@
     row = lax.broadcasted_iota(jnp.int32, (PAGE, HEAD), 0).astype(F32).astype(BF16)
     last = row == jnp.asarray(PAGE - 1, BF16)
     zero = jnp.zeros((PAGE, HEAD), BF16)
-
-    def splat(value):
-        return jnp.full((1, HEAD), value, F32)
+    tile_row = lax.broadcasted_iota(jnp.int32, (TILE, HEAD), 0).astype(F32)
 
     def move(k):
         peer = partner(k)
@@ -158,23 +158,14 @@
         length = lens[request].astype(F32)
         flag = mig[request].astype(F32)
         rows_new = fresh[request].astype(F32)
-        for p in range(2):
-            at = splat(length - p * PAGE).astype(BF16)
-            next_at = splat(length - p * PAGE + 1.0).astype(BF16)
-            keep = row < at
-            first = row == at
-            second = row == next_at
-            for c in range(2):
-                page = pool[table[p, request], c]
-                new0 = rows_new[0, c : c + 1].astype(BF16)
-                new1 = rows_new[1, c : c + 1].astype(BF16)
-                block = jnp.where(keep, page, zero)
-                block = jnp.where(first, new0, block)
-                block = jnp.where(second, new1, block)
-                if p == 1:
-                    note = splat(length if c == 0 else flag).astype(BF16)
-                    block = jnp.where(last, note, block)
-                ref[slot, p, c] = block
+        for c in range(2):
+            ref[slot, 0, c] = pool[table[0, request], c]
+            page = pool[table[1, request], c]
+            ref[slot, 1, c, : PAGE - TILE] = page[: PAGE - TILE]
+            end = jnp.where(tile_row == TILE - 3.0, rows_new[0, c : c + 1], page[PAGE - TILE :].astype(F32))
+            end = jnp.where(tile_row == TILE - 2.0, rows_new[1, c : c + 1], end)
+            end = jnp.where(tile_row == TILE - 1.0, length if c == 0 else flag, end)
+            ref[slot, 1, c, PAGE - TILE :] = end.astype(BF16)
 
     q_wide = qsrc[...].astype(F32)
     for g in range(GROUPS):
@@ -193,9 +184,16 @@
         return 0
 
     batch = min(4, n)
-    lax.fori_loop(1, n, send_step, 0)
+    ahead = min(4 * batch, n)
+    lax.fori_loop(1, ahead, send_step, 0)
     pack(0, send)
     arr[me] = send[me]
+
+    def pack_step(k, _):
+        pack(k, send)
+        return 0
+
+    lax.fori_loop(ahead, n, pack_step, 0)
 
     def dot_t(a, b):
         return lax.dot_general(a, b, (((1,), (1,)), ((), ())), preferred_element_type=F32)
@@ -214,6 +212,7 @@
     wide = min(8, n)
     lane8 = lax.broadcasted_iota(jnp.int32, (8, HEAD), 1)
     step8 = lax.broadcasted_iota(jnp.int32, (8, HEAD), 0) % 2
+    fresh8 = (lane8 == PAGE - 3) | ((lane8 == PAGE - 2) & (step8 == 1))
 
     def src_step(b, _):
         parts0, parts1 = [], []
@@ -221,18 +220,17 @@
             request = b * wide + i
             slot = tgts[request]
             query = qs[request].astype(BF16)
-            bound = lens[request] + 1 + step8
+            bound = lens[request]
             s0 = dot_t(query, send[slot, 0, 0]) * scale
             s1 = dot_t(query, send[slot, 1, 0]) * scale
             parts0.append(jnp.where(lane8 < bound, s0, NEG))
-            parts1.append(jnp.where(lane8 + PAGE < bound, s1, NEG))
+            parts1.append(jnp.where((lane8 + PAGE < bound) | fresh8, s1, NEG))
         w0, w1 = soft(jnp.concatenate(parts0, axis=0), jnp.concatenate(parts1, axis=0))
         for i in range(wide):
             request = b * wide + i
             slot = tgts[request]
             rows = slice(8 * i, 8 * i + 8)
-            value1 = jnp.where(last, zero, send[slot, 1, 1])
-            mixed = dot(w0[rows], send[slot, 0, 1]) + dot(w1[rows], value1)
+            mixed = dot(w0[rows], send[slot, 0, 1]) + dot(w1[rows], send[slot, 1, 1])
             for g in range(GROUPS):
                 att_s[g, pl.ds(2 * request, 2), :] = mixed[2 * g : 2 * g + 2]
         return 0
@@ -431,6 +429,11 @@
 
     lane4 = lax.broadcasted_iota(jnp.int32, (GROUPS, HEAD), 1).astype(F32)
 
+    def state(slot):
+        length = arr[slot, 1, 0, PAGE - TILE :].astype(F32)[TILE - 1 :]
+        flag = arr[slot, 1, 1, PAGE - TILE :].astype(F32)[TILE - 1 :]
+        return length, flag == 1.0
+
     def dst_step(b, _):
         slots, parts0, parts1, values = [], [], [], []
         for i in range(batch):
@@ -440,70 +443,101 @@
             def _():
                 move(k).wait_send()
 
+            @pl.when(k + ahead < n)
+            def _():
+                move(k + ahead).start()
+
         for i in range(batch):
             k = b * batch + i
-            slot = partner(k)
-            slots.append(slot)
 
             @pl.when(k > 0)
             def _():
                 arrive(k).wait_recv()
 
-            length = arr[slot, 1, 0][PAGE - 1 :].astype(F32)
-            flag = arr[slot, 1, 1][PAGE - 1 :].astype(F32)
-            moved = jnp.broadcast_to(flag, (PAGE, HEAD)).astype(BF16) == jnp.asarray(1.0, BF16)
+        for i in range(batch):
+            slot = partner(b * batch + i)
+            slots.append(slot)
+            length, moved = state(slot)
             own = rdst[slot].astype(F32)
-            kept = []
-            for p in range(2):
-                at = (length + (2.0 - p * PAGE)).astype(BF16)
-                hit = row == at
-                for c in range(2):
-                    block = arr[slot, p, c]
-                    if p == 1:
-                        block = jnp.where(last, zero, block)
-                    block = jnp.where(hit, own[c : c + 1].astype(BF16), block)
-                    block = jnp.where(moved, block, zero)
-                    cache_out[slot, p, c] = block
-                    kept.append(block)
+            key1 = jnp.where(last, own[0:1].astype(BF16), arr[slot, 1, 0])
+            value1 = jnp.where(last, own[1:2].astype(BF16), arr[slot, 1, 1])
             query = qd[slot].astype(BF16)
-            bound = length + 3.0
-            s0 = dot_t(query, kept[0]) * scale
-            s1 = dot_t(query, kept[2]) * scale
-            parts0.append(jnp.where(lane4 < bound, s0, NEG))
-            parts1.append(jnp.where(lane4 + float(PAGE) < bound, s1, NEG))
-            values.append((kept[1], kept[3]))
+            s0 = dot_t(query, arr[slot, 0, 0]) * scale
+            s1 = dot_t(query, key1) * scale
+            parts0.append(jnp.where(lane4 < length, s0, NEG))
+            keep1 = (lane4 + float(PAGE) < length) | (lane4 >= PAGE - 3.0)
+            parts1.append(jnp.where(keep1, s1, NEG))
+            values.append((arr[slot, 0, 1], value1, moved))
         for i in range(batch):
             w0, w1 = soft(parts0[i], parts1[i])
             mixed = dot(w0, values[i][0]) + dot(w1, values[i][1])
+            mixed = jnp.where(values[i][2], mixed, 0.0)
             for g in range(GROUPS):
                 att_d[g, pl.ds(slots[i], 1), :] = mixed[g : g + 1]
         return 0
 
+    def fill_step(b, _):
+        for i in range(batch):
+            slot = partner(b * batch + i)
+            length, moved = state(slot)
+            length = jnp.where(moved, length, -512.0)
+            own = rdst[slot].astype(F32)
+            rows_in = [arr[slot, 1, c, PAGE - TILE :].astype(F32) for c in range(2)]
+            for p in range(2):
+                at = [(length + (j - p * PAGE)).astype(BF16) for j in range(3)]
+                keep = row < at[0]
+                hits = [row == spot for spot in at]
+                for c in range(2):
+                    rows_put = [
+                        rows_in[c][TILE - 3 : TILE - 2],
+                        rows_in[c][TILE - 2 : TILE - 1],
+                        own[c : c + 1],
+                    ]
+                    block = jnp.where(keep, arr[slot, p, c], zero)
+                    for hit, put in zip(hits, rows_put):
+                        block = jnp.where(hit, put.astype(BF16), block)
+                    cache_out[slot, p, c] = block
+        return 0
+
+    def both(b, _):
+        dst_step(b, 0)
+        return fill_step(b, 0)
+
     steps = n // batch
-    marks = [steps * j // 8 for j in (0, 2, 4, 6, 8)]
-    lax.fori_loop(marks[0], marks[1], dst_step, 0)
+    marks = [steps * j // 8 for j in (0, 1, 3, 5, 6, 7, 8)]
+    lax.fori_loop(marks[0], marks[1], both, 0)
     far()
-    lax.fori_loop(marks[1], marks[2], dst_step, 0)
+    lax.fori_loop(marks[1], marks[2], both, 0)
     close()
-    lax.fori_loop(marks[2], marks[3], dst_step, 0)
+    lax.fori_loop(marks[2], marks[3], both, 0)
     total_up()
-    lax.fori_loop(marks[3], marks[4], dst_step, 0)
+    lax.fori_loop(marks[3], marks[4], both, 0)
+    lax.fori_loop(marks[4], marks[6], dst_step, 0)
 
     dst_tail = tail(1, att_d, d_half, d_half_in, d_pair, d_rs, d_rs_in, d_full)
     dst_tail[0]()
     relay()
-    for stage in dst_tail[1:]:
-        stage()
+    dst_tail[1]()
+    lax.fori_loop(marks[4], marks[5], fill_step, 0)
+    dst_tail[2]()
+    lax.fori_loop(marks[5], marks[6], fill_step, 0)
+    dst_tail[3]()
     end()
-
-
-def place(*refs):
-    sem = refs[-1]
-    half = len(refs) // 2
+    dst_tail[4]()
+
+
+def place(src_in, cache_in, dst_in, src_hbm, cache_hbm, dst_hbm, sem):
+    size = cache_in.shape[0] // PIECES
     copies = [
-        pltpu.make_async_copy(src, dst, sem.at[i])
-        for i, (src, dst) in enumerate(zip(refs[:half], refs[half:-1]))
+        pltpu.make_async_copy(
+            cache_in.at[i * size : (i + 1) * size],
+            cache_hbm.at[i * size : (i + 1) * size],
+            sem.at[i],
+        )
+        for i in range(PIECES)
     ]
+    copies.append(pltpu.make_async_copy(src_in, src_hbm, sem.at[PIECES]))
+    copies.append(pltpu.make_async_copy(dst_in, dst_hbm, sem.at[PIECES + 1]))
     for copy in copies:
         copy.start()
     for copy in copies:
@@ -598,7 +632,7 @@
         out_shape=tuple(pltpu.HBM(x.shape, x.dtype) for x in results),
         in_specs=[vmem] * 3,
         out_specs=(hbm,) * 3,
-        scratch_shapes=[dma((3,))],
+        scratch_shapes=[dma((PIECES + 2,))],
         compiler_params=pltpu.CompilerParams(vmem_limit_bytes=8 * 1024 * 1024),
         name="place",
     )(*(pltpu.with_memory_space_constraint(x, pltpu.VMEM) for x in results))

time: 93.2 us -> 90.5 us (0.971); the launches traced: 91.7 us -> 90.4 us
  Pallas kernels: 91.1 us -> 89.8 us
    pallas_call x1, Pallas kernels: 88.8 us -> 87.4 us  [shards(): pl.pallas_call(functools.partial(kernel, n, tp_size), out_shape=(pltpu.VM...]
where the time goes in v4:
time: 90.5 us; the launch traced here: 90.4 us
  Pallas kernels  89.8 us (99%)
    pallas_call x1, Pallas kernels, shards(): pl.pallas_call(functools.partial(kernel, n, tp_size), out_shape=(pltpu.VM...  87.4 us
    pallas_call x1, Pallas kernels, shards(): pl.pallas_call(place, out_shape=tuple((pltpu.HBM(x.shape, x.dtype) for x...  2.33 us

profile of v4, /device:TPU:1, one launch (start us, length us, event | category | flops | bytes accessed | tf_op | source)
XLA Modules:
  0.0 90.4 jit_solution(7689846973690109007)
XLA Ops:
  0.6 87.4 %migrate.1 = (bf16[32,2,4096]{2,1,0:T(2,128)(2,1)S(1)}, bf16[32,2,2,128,128]{4,3,2,1,0:T(8,128)(2,1)S(1)}, bf16[32,4096]{1,0:T(8,128)(2,1)S(1)}) custom-call(s32[32]{0:T(128)} %lens.1, s32[32]{0:T(128)} %tgts.1, s32[32]{0:T(128)} %mig.1, s32[2,32]{1,0:T(2,128)} %bitcast.1, bf16[32,2,512]{2,1,0:T(2,128)(2,1)} %qsrc.1, bf16[32,2,2,128]{3,2,1,0:T(2,128)(2,1)} %fresh.1, ...), custom_call_target="tpu_custom_call" | custom-call | tf_op jit(solution)/shard_map/migrate/pallas_call | solution.py:579
  88.1 2.3 %place.1 = (bf16[32,2,4096]{2,1,0:T(2,128)(2,1)}, bf16[32,2,2,128,128]{4,3,2,1,0:T(8,128)(2,1)}, bf16[32,4096]{1,0:T(8,128)(2,1)}) custom-call(bf16[32,2,4096]{2,1,0:T(2,128)(2,1)S(1)} %get-tuple-element.6.src_in, bf16[32,2,2,128,128]{4,3,2,1,0:T(8,128)(2,1)S(1)} %get-tuple-element.7.cache_in, bf16[32,4096]{1,0:T(8,128)(2,1)S(1)} %get-tuple-element.8.dst_in), custom_call_target="tpu_custom_call" | custom-call | tf_op jit(solution)/shard_map/place/pallas_call | solution.py:630

commit v5 on v4

--- a/solution.py
+++ b/solution.py
@@ -62,7 +62,7 @@
     w_hbm,
     s_full,
     cache_out,
-    d_full,
+    d_out,
     pool,
     w,
     send,
@@ -78,11 +78,18 @@
     s_cross_in,
     s_rs,
     s_rs_in,
-    d_half,
-    d_half_in,
-    d_pair,
-    d_rs,
-    d_rs_in,
+    e_half,
+    e_half_in,
+    e_pair,
+    e_rs,
+    e_rs_in,
+    e_full,
+    d_early,
+    l_half,
+    l_half_in,
+    l_pair,
+    l_parts,
+    l_final,
     load_sem,
     send_sem,
     recv_sem,
@@ -90,6 +97,7 @@
     rs_sem,
     ag_sem,
     fwd_sem,
+    late_sem,
 ):
     me = lax.axis_index("inst")
     tp = lax.axis_index("tp")
@@ -99,6 +107,8 @@
     mate = tp + 1 - 2 * core
     bits = n.bit_length() - 1
     scale = 1.0 / math.sqrt(HEAD)
+    early_rows = n * 3 // 4
+    late_rows = n - early_rows
     cols = w.shape[1] // tp_size
 
     def peer_hi(step):
@@ -344,49 +354,41 @@
 
         return project, far, close, total, relay, end
 
-    def tail(part, att, half, half_in, pair, rs, rs_in, full):
-        a = jnp.concatenate([att[g].astype(BF16) for g in range(GROUPS)], axis=1)
-
-        def part_full(index):
-            where = block_cols(index)
-            return full.at[:, where]
-
-        swap = remote(half, half_in, half_sem, part, mate)
+    def stack(x, parts):
+        size = x.shape[1] // parts
+        return jnp.concatenate([x[:, i * size : (i + 1) * size] for i in range(parts)], axis=0)
+
+    def rows_of(att, rows):
+        return jnp.concatenate([att[g, rows].astype(BF16) for g in range(GROUPS)], axis=1)
+
+    def early_tail(att, half, half_in, pair, rs, rs_in, full):
+        a = rows_of(att, slice(0, early_rows))
+        swap = remote(half, half_in, half_sem, 1, mate)
         scatter = [
-            remote(rs.at[step], rs_in.at[step], rs_sem, part * his + step, peer_hi(step))
+            remote(rs.at[step], rs_in.at[step], rs_sem, his + step, peer_hi(step))
             for step in range(1, his)
         ]
-        mine = part_full(tp)
-        gather = [
-            remote(mine, mine, ag_sem, part * his + step, peer_hi(step))
+        mine = full.at[tp]
+        owners = [((hi + his - step) % his) * 2 for step in range(his)]
+        gather = [remote(mine, mine, ag_sem, his + step, peer_hi(step)) for step in range(1, his)]
+        landed = [
+            remote(mine, full.at[owners[step] + core], ag_sem, his + step, peer_hi(step))
             for step in range(1, his)
         ]
-        landed = [
-            remote(
-                mine,
-                part_full(((hi + his - step) % his) * 2 + core),
-                ag_sem,
-                part * his + step,
-                peer_hi(step),
-            )
-            for step in range(1, his)
-        ]
-        forward = []
-        received = []
+        forward, received = [], []
         for step in range(his):
-            owner = ((hi + his - step) % his) * 2
-            have, want = part_full(owner + core), part_full(owner + 1 - core)
-            forward.append(remote(have, have, fwd_sem, part * his + step, mate))
-            received.append(remote(have, want, fwd_sem, part * his + step, mate))
+            have, want = full.at[owners[step] + core], full.at[owners[step] + 1 - core]
+            forward.append(remote(have, have, fwd_sem, his + step, mate))
+            received.append(remote(have, want, fwd_sem, his + step, mate))
 
         def one():
             for step in range(his):
                 z = (hi + step) % his
-                half[step] = dot(a, w[:, block_cols(z * 2 + 1 - core)]).astype(BF16)
+                half[step] = stack(dot(a, w[:, block_cols(z * 2 + 1 - core)]), 2).astype(BF16)
             swap.start()
             for step in range(his):
                 z = (hi + step) % his
-                pair[step] = dot(a, w[:, block_cols(z * 2 + core)])
+                pair[step] = stack(dot(a, w[:, block_cols(z * 2 + core)]), 2)
 
         def two():
             swap.wait()
@@ -410,16 +412,70 @@
             for step in range(1, his):
                 landed[step - 1].wait_recv()
                 forward[step].start()
-            for step in range(his):
-                received[step].wait_recv()
 
         def five():
-            for copy in gather:
+            for copy in received:
+                copy.wait_recv()
+            for copy in gather + forward:
                 copy.wait_send()
-            for copy in forward:
+
+        return one, two, three, four, five
+
+    def late_tail(att, half, half_in, pair, parts, final):
+        a = rows_of(att, slice(early_rows, n))
+        swap = remote(half, half_in, late_sem, 0, mate)
+        spread_out = [
+            remote(parts.at[hi], parts.at[hi], late_sem, step, peer_hi(step))
+            for step in range(1, his)
+        ]
+        spread_in = [
+            remote(parts.at[hi], parts.at[(hi + his - step) % his], late_sem, step, peer_hi(step))
+            for step in range(1, his)
+        ]
+        give = remote(final.at[core], final.at[core], late_sem, his, mate)
+        take = remote(final.at[core], final.at[1 - core], late_sem, his, mate)
+
+        def columns(side):
+            blocks = [dot(a, w[:, block_cols(z * 2 + side)]) for z in range(his)]
+            return stack(jnp.concatenate(blocks, axis=1), 2)
+
+        def one():
+            half[...] = columns(1 - core).astype(BF16)
+            swap.start()
+            pair[...] = columns(core)
+
+        def two():
+            swap.wait()
+            parts[hi] = (pair[...] + half_in[...].astype(F32)).astype(BF16)
+            for copy in spread_out:
+                copy.start()
+
+        def three():
+            for copy in spread_in:
+                copy.wait_recv()
+            total = parts[0].astype(F32)
+            for z in range(1, his):
+                total = total + parts[z].astype(F32)
+            final[core] = total.astype(BF16)
+            give.start()
+
+        def four():
+            take.wait_recv()
+
+        def five():
+            for copy in spread_out:
                 copy.wait_send()
+            give.wait_send()
 
         return one, two, three, four, five
+
+    def one_hot(first, count, skip):
+        lane = lax.broadcasted_iota(jnp.int32, (n, HEAD), 1)
+        owner = jnp.full((n, HEAD), -1, jnp.int32)
+        for i in range(count):
+            owner = jnp.where(lane == skip + i, partner(first + i), owner)
+        hit = lax.broadcasted_iota(jnp.int32, (n, HEAD), 0) == owner
+        return jnp.where(hit, 1.0, 0.0).astype(BF16)[:, : 2 * count]
 
     load_w.wait()
     project, far, close, total_up, relay, end = ring_tail(
@@ -435,7 +491,7 @@
         return length, flag == 1.0
 
     def dst_step(b, _):
-        slots, parts0, parts1, values = [], [], [], []
+        parts0, parts1, values = [], [], []
         for i in range(batch):
             k = b * batch + i
 
@@ -456,7 +512,6 @@
 
         for i in range(batch):
             slot = partner(b * batch + i)
-            slots.append(slot)
             length, moved = state(slot)
             own = rdst[slot].astype(F32)
             key1 = jnp.where(last, own[0:1].astype(BF16), arr[slot, 1, 0])
@@ -473,7 +528,7 @@
             mixed = dot(w0, values[i][0]) + dot(w1, values[i][1])
             mixed = jnp.where(values[i][2], mixed, 0.0)
             for g in range(GROUPS):
-                att_d[g, pl.ds(slots[i], 1), :] = mixed[g : g + 1]
+                att_d[g, pl.ds(b * batch + i, 1), :] = mixed[g : g + 1]
         return 0
 
     def fill_step(b, _):
@@ -511,19 +566,41 @@
     close()
     lax.fori_loop(marks[2], marks[3], both, 0)
     total_up()
-    lax.fori_loop(marks[3], marks[4], both, 0)
-    lax.fori_loop(marks[4], marks[6], dst_step, 0)
-
-    dst_tail = tail(1, att_d, d_half, d_half_in, d_pair, d_rs, d_rs_in, d_full)
-    dst_tail[0]()
+    lax.fori_loop(marks[3], marks[4], dst_step, 0)
+    early = early_tail(att_d, e_half, e_half_in, e_pair, e_rs, e_rs_in, e_full)
+    early[0]()
+    early[1]()
+    lax.fori_loop(marks[4], marks[5], dst_step, 0)
+    early[2]()
     relay()
-    dst_tail[1]()
-    lax.fori_loop(marks[4], marks[5], fill_step, 0)
-    dst_tail[2]()
-    lax.fori_loop(marks[5], marks[6], fill_step, 0)
-    dst_tail[3]()
+    lax.fori_loop(marks[5], marks[6], dst_step, 0)
+    late = late_tail(att_d, l_half, l_half_in, l_pair, l_parts, l_final)
+    late[0]()
+    early[3]()
+    late[1]()
+    lax.fori_loop(marks[3], marks[6], fill_step, 0)
+    early[4]()
+    size = cols // 2
+    for side in range(2):
+        spots = one_hot(0, early_rows, side * early_rows)
+        for index in range(tp_size):
+            start = index * cols + side * size
+            d_early[:, start : start + size] = dot(spots, e_full[index])
+    late_spots = [one_hot(early_rows, late_rows, side * late_rows) for side in range(2)]
+
+    def set_out(side):
+        for z in range(his):
+            where = block_cols(z * 2 + side)
+            have = l_final[side, :, (z % 2) * cols : (z % 2 + 1) * cols]
+            rows_late = dot(late_spots[z // (his // 2)], have)
+            d_out[:, where] = (d_early[:, where] + rows_late).astype(BF16)
+
+    late[2]()
+    set_out(core)
+    late[3]()
+    set_out(1 - core)
     end()
-    dst_tail[4]()
+    late[4]()
 
 
 def place(src_in, cache_in, dst_in, src_hbm, cache_hbm, dst_hbm, sem):
@@ -566,6 +643,8 @@
     vmem = pl.BlockSpec(memory_space=pltpu.VMEM)
     hbm = pl.BlockSpec(memory_space=pl.ANY)
     cache = (requests, 2, 2, PAGE, HEAD)
+    early = (requests // 4 * 6, cols // 2)
+    late = (requests // 4 * 2, width // 4)
 
     def sums(rows, sent):
         return [
@@ -596,7 +675,20 @@
             pltpu.VMEM((GROUPS, requests, HEAD), F32),
         ]
         + sums(2 * requests, [(2, cols // 2)] * 2 + [(2, cols)] * 2)
-        + sums(requests, [(his, cols)] * 2)
+        + [
+            pltpu.VMEM((his,) + early, BF16),
+            pltpu.VMEM((his,) + early, BF16),
+            pltpu.VMEM((his,) + early, F32),
+            pltpu.VMEM((his,) + early, BF16),
+            pltpu.VMEM((his,) + early, BF16),
+            pltpu.VMEM((tp_size,) + early, BF16),
+            pltpu.VMEM((requests, width), F32),
+            pltpu.VMEM(late, BF16),
+            pltpu.VMEM(late, BF16),
+            pltpu.VMEM(late, F32),
+            pltpu.VMEM((his,) + late, BF16),
+            pltpu.VMEM((2,) + late, BF16),
+        ]
         + [
             dma((2,)),
             dma((n,)),
@@ -605,6 +697,7 @@
             dma((4 * his,)),
             dma((4 * his,)),
             dma((4 * his,)),
+            dma((2 * his + 2,)),
         ],
         compiler_params=pltpu.CompilerParams(
             collective_id=0, has_side_effects=True, vmem_limit_bytes=28 * 1024 * 1024

time: 90.5 us -> 93.2 us (1.030)
  Pallas kernels: 89.8 us -> 92.4 us
    pallas_call x1, Pallas kernels: 87.4 us -> 90.1 us  [shards(): pl.pallas_call(functools.partial(kernel, n, tp_size), out_shape=(pltpu.VM...]
where the time goes in v5:
time: 93.2 us; the launch traced here: 93.1 us
  Pallas kernels  92.4 us (99%)
    pallas_call x1, Pallas kernels, shards(): pl.pallas_call(functools.partial(kernel, n, tp_size), out_shape=(pltpu.VM...  90.1 us
    pallas_call x1, Pallas kernels, shards(): pl.pallas_call(place, out_shape=tuple((pltpu.HBM(x.shape, x.dtype) for x...  2.33 us

profile of v5, /device:TPU:1, one launch (start us, length us, event | category | flops | bytes accessed | tf_op | source)
XLA Modules:
  0.0 93.1 jit_solution(1322385708915204952)
XLA Ops:
  0.6 90.1 %migrate.1 = (bf16[32,2,4096]{2,1,0:T(2,128)(2,1)S(1)}, bf16[32,2,2,128,128]{4,3,2,1,0:T(8,128)(2,1)S(1)}, bf16[32,4096]{1,0:T(8,128)(2,1)S(1)}) custom-call(s32[32]{0:T(128)} %lens.1, s32[32]{0:T(128)} %tgts.1, s32[32]{0:T(128)} %mig.1, s32[2,32]{1,0:T(2,128)} %bitcast.1, bf16[32,2,512]{2,1,0:T(2,128)(2,1)} %qsrc.1, bf16[32,2,2,128]{3,2,1,0:T(2,128)(2,1)} %fresh.1, ...), custom_call_target="tpu_custom_call" | custom-call | tf_op jit(solution)/shard_map/migrate/pallas_call | solution.py:658
  90.8 2.3 %place.1 = (bf16[32,2,4096]{2,1,0:T(2,128)(2,1)}, bf16[32,2,2,128,128]{4,3,2,1,0:T(8,128)(2,1)}, bf16[32,4096]{1,0:T(8,128)(2,1)}) custom-call(bf16[32,2,4096]{2,1,0:T(2,128)(2,1)S(1)} %get-tuple-element.6.src_in, bf16[32,2,2,128,128]{4,3,2,1,0:T(8,128)(2,1)S(1)} %get-tuple-element.7.cache_in, bf16[32,4096]{1,0:T(8,128)(2,1)S(1)} %get-tuple-element.8.dst_in), custom_call_target="tpu_custom_call" | custom-call | tf_op jit(solution)/shard_map/place/pallas_call | solution.py:723

commit v6 on v4

--- a/solution.py
+++ b/solution.py
@@ -139,6 +139,19 @@
             device_id_type=MESH,
         )
 
+    def launch(k):
+        peer = partner(k)
+        for p in range(2):
+            for c in range(2):
+                pltpu.make_async_remote_copy(
+                    src_ref=send.at[peer, p, c],
+                    dst_ref=arr.at[me, p, c],
+                    send_sem=send_sem.at[k],
+                    recv_sem=recv_sem.at[k],
+                    device_id=(peer, tp),
+                    device_id_type=MESH,
+                ).start()
+
     def arrive(k):
         peer = partner(k)
         return pltpu.make_async_remote_copy(
@@ -175,25 +188,30 @@
         qd[:, g, :] = qdst[:, lanes].astype(F32)
 
     load_pool.wait()
-    pl.semaphore_wait(barrier, n - 1 + his)
     load_w.start()
 
     def send_step(k, _):
         pack(k, send)
-        move(k).start()
+        launch(k)
         return 0
 
-    batch = min(4, n)
-    ahead = min(4 * batch, n)
-    lax.fori_loop(1, ahead, send_step, 0)
-    pack(0, send)
-    arr[me] = send[me]
+    def launch_step(k, _):
+        launch(k)
+        return 0
 
     def pack_step(k, _):
         pack(k, send)
         return 0
 
+    batch = min(4, n)
+    ahead = min(4 * batch, n)
+    ready = min(9, n)
+    lax.fori_loop(0, ready, pack_step, 0)
+    pl.semaphore_wait(barrier, n - 1 + his)
+    lax.fori_loop(1, ready, launch_step, 0)
+    lax.fori_loop(ready, ahead, send_step, 0)
     lax.fori_loop(ahead, n, pack_step, 0)
+    arr[me] = send[me]
 
     def dot_t(a, b):
         return lax.dot_general(a, b, (((1,), (1,)), ((), ())), preferred_element_type=F32)
@@ -445,7 +463,7 @@
 
             @pl.when(k + ahead < n)
             def _():
-                move(k + ahead).start()
+                launch(k + ahead)
 
         for i in range(batch):
             k = b * batch + i

time: 90.5 us -> 90 us (level)
  no operation moved by 1% of the time
where the time goes in v6:
time: 90 us; the launch traced here: 89.9 us
  Pallas kernels  89.3 us (99%)
    pallas_call x1, Pallas kernels, shards(): pl.pallas_call(functools.partial(kernel, n, tp_size), out_shape=(pltpu.VM...  86.9 us
    pallas_call x1, Pallas kernels, shards(): pl.pallas_call(place, out_shape=tuple((pltpu.HBM(x.shape, x.dtype) for x...  2.33 us

profile of v6, /device:TPU:1, one launch (start us, length us, event | category | flops | bytes accessed | tf_op | source)
XLA Modules:
  0.0 89.9 jit_solution(6075538588681949660)
XLA Ops:
  0.6 86.9 %migrate.1 = (bf16[32,2,4096]{2,1,0:T(2,128)(2,1)S(1)}, bf16[32,2,2,128,128]{4,3,2,1,0:T(8,128)(2,1)S(1)}, bf16[32,4096]{1,0:T(8,128)(2,1)S(1)}) custom-call(s32[32]{0:T(128)} %lens.1, s32[32]{0:T(128)} %tgts.1, s32[32]{0:T(128)} %mig.1, s32[2,32]{1,0:T(2,128)} %bitcast.1, bf16[32,2,512]{2,1,0:T(2,128)(2,1)} %qsrc.1, bf16[32,2,2,128]{3,2,1,0:T(2,128)(2,1)} %fresh.1, ...), custom_call_target="tpu_custom_call" | custom-call | tf_op jit(solution)/shard_map/migrate/pallas_call | solution.py:597
  87.6 2.3 %place.1 = (bf16[32,2,4096]{2,1,0:T(2,128)(2,1)}, bf16[32,2,2,128,128]{4,3,2,1,0:T(8,128)(2,1)}, bf16[32,4096]{1,0:T(8,128)(2,1)}) custom-call(bf16[32,2,4096]{2,1,0:T(2,128)(2,1)S(1)} %get-tuple-element.6.src_in, bf16[32,2,2,128,128]{4,3,2,1,0:T(8,128)(2,1)S(1)} %get-tuple-element.7.cache_in, bf16[32,4096]{1,0:T(8,128)(2,1)S(1)} %get-tuple-element.8.dst_in), custom_call_target="tpu_custom_call" | custom-call | tf_op jit(solution)/shard_map/place/pallas_call | solution.py:648

commit v7 on v6

--- a/solution.py
+++ b/solution.py
@@ -522,25 +522,23 @@
         return fill_step(b, 0)
 
     steps = n // batch
-    marks = [steps * j // 8 for j in (0, 1, 3, 5, 6, 7, 8)]
+    marks = [steps * j // 8 for j in (0, 2, 5, 6, 7, 8)]
     lax.fori_loop(marks[0], marks[1], both, 0)
     far()
     lax.fori_loop(marks[1], marks[2], both, 0)
     close()
-    lax.fori_loop(marks[2], marks[3], both, 0)
-    total_up()
-    lax.fori_loop(marks[3], marks[4], both, 0)
-    lax.fori_loop(marks[4], marks[6], dst_step, 0)
+    lax.fori_loop(marks[2], marks[5], dst_step, 0)
 
     dst_tail = tail(1, att_d, d_half, d_half_in, d_pair, d_rs, d_rs_in, d_full)
     dst_tail[0]()
+    total_up()
+    dst_tail[1]()
+    lax.fori_loop(marks[2], marks[4], fill_step, 0)
     relay()
-    dst_tail[1]()
+    dst_tail[2]()
     lax.fori_loop(marks[4], marks[5], fill_step, 0)
-    dst_tail[2]()
-    lax.fori_loop(marks[5], marks[6], fill_step, 0)
+    end()
     dst_tail[3]()
-    end()
     dst_tail[4]()
 
 

time: 90 us -> 91.9 us (1.021)
  Pallas kernels: 89.3 us -> 91.1 us
    pallas_call x1, Pallas kernels: 86.9 us -> 88.8 us  [shards(): pl.pallas_call(functools.partial(kernel, n, tp_size), out_shape=(pltpu.VM...]
where the time goes in v7:
time: 91.9 us; the launch traced here: 91.7 us
  Pallas kernels  91.1 us (99%)
    pallas_call x1, Pallas kernels, shards(): pl.pallas_call(functools.partial(kernel, n, tp_size), out_shape=(pltpu.VM...  88.8 us
    pallas_call x1, Pallas kernels, shards(): pl.pallas_call(place, out_shape=tuple((pltpu.HBM(x.shape, x.dtype) for x...  2.33 us

profile of v7, /device:TPU:1, one launch (start us, length us, event | category | flops | bytes accessed | tf_op | source)
XLA Modules:
  0.0 91.7 jit_solution(14790772716120680787)
XLA Ops:
  0.6 88.8 %migrate.1 = (bf16[32,2,4096]{2,1,0:T(2,128)(2,1)S(1)}, bf16[32,2,2,128,128]{4,3,2,1,0:T(8,128)(2,1)S(1)}, bf16[32,4096]{1,0:T(8,128)(2,1)S(1)}) custom-call(s32[32]{0:T(128)} %lens.1, s32[32]{0:T(128)} %tgts.1, s32[32]{0:T(128)} %mig.1, s32[2,32]{1,0:T(2,128)} %bitcast.1, bf16[32,2,512]{2,1,0:T(2,128)(2,1)} %qsrc.1, bf16[32,2,2,128]{3,2,1,0:T(2,128)(2,1)} %fresh.1, ...), custom_call_target="tpu_custom_call" | custom-call | tf_op jit(solution)/shard_map/migrate/pallas_call | solution.py:595
  89.4 2.3 %place.1 = (bf16[32,2,4096]{2,1,0:T(2,128)(2,1)}, bf16[32,2,2,128,128]{4,3,2,1,0:T(8,128)(2,1)}, bf16[32,4096]{1,0:T(8,128)(2,1)}) custom-call(bf16[32,2,4096]{2,1,0:T(2,128)(2,1)S(1)} %get-tuple-element.6.src_in, bf16[32,2,2,128,128]{4,3,2,1,0:T(8,128)(2,1)S(1)} %get-tuple-element.7.cache_in, bf16[32,4096]{1,0:T(8,128)(2,1)S(1)} %get-tuple-element.8.dst_in), custom_call_target="tpu_custom_call" | custom-call | tf_op jit(solution)/shard_map/place/pallas_call | solution.py:646

commit v8 on v7

--- a/solution.py
+++ b/solution.py
@@ -209,8 +209,7 @@
     lax.fori_loop(0, ready, pack_step, 0)
     pl.semaphore_wait(barrier, n - 1 + his)
     lax.fori_loop(1, ready, launch_step, 0)
-    lax.fori_loop(ready, ahead, send_step, 0)
-    lax.fori_loop(ahead, n, pack_step, 0)
+    lax.fori_loop(ready, n, pack_step, 0)
     arr[me] = send[me]
 
     def dot_t(a, b):
@@ -443,7 +442,10 @@
     project, far, close, total_up, relay, end = ring_tail(
         att_s, s_half, s_half_in, s_pair, s_cross, s_cross_in, s_rs, s_rs_in, s_full
     )
+    lax.fori_loop(ready, ready + 2, launch_step, 0)
     project()
+    far()
+    lax.fori_loop(ready + 2, ahead, launch_step, 0)
 
     lane4 = lax.broadcasted_iota(jnp.int32, (GROUPS, HEAD), 1).astype(F32)
 
@@ -522,24 +524,23 @@
         return fill_step(b, 0)
 
     steps = n // batch
-    marks = [steps * j // 8 for j in (0, 2, 5, 6, 7, 8)]
+    marks = [steps * j // 8 for j in (0, 2, 4, 6, 7, 8)]
     lax.fori_loop(marks[0], marks[1], both, 0)
-    far()
+    close()
     lax.fori_loop(marks[1], marks[2], both, 0)
-    close()
-    lax.fori_loop(marks[2], marks[5], dst_step, 0)
+    total_up()
+    lax.fori_loop(marks[2], marks[3], both, 0)
+    relay()
+    lax.fori_loop(marks[3], marks[5], dst_step, 0)
 
     dst_tail = tail(1, att_d, d_half, d_half_in, d_pair, d_rs, d_rs_in, d_full)
     dst_tail[0]()
-    total_up()
+    lax.fori_loop(marks[3], marks[4], fill_step, 0)
     dst_tail[1]()
-    lax.fori_loop(marks[2], marks[4], fill_step, 0)
-    relay()
-    dst_tail[2]()
     lax.fori_loop(marks[4], marks[5], fill_step, 0)
     end()
-    dst_tail[3]()
-    dst_tail[4]()
+    for stage in dst_tail[2:]:
+        stage()
 
 
 def place(src_in, cache_in, dst_in, src_hbm, cache_hbm, dst_hbm, sem):

time: 91.9 us -> 91.9 us (level)
  no operation moved by 1% of the time
where the time goes in v8:
time: 91.9 us; the launch traced here: 91.8 us
  Pallas kernels  91.1 us (99%)
    pallas_call x1, Pallas kernels, shards(): pl.pallas_call(functools.partial(kernel, n, tp_size), out_shape=(pltpu.VM...  88.8 us
    pallas_call x1, Pallas kernels, shards(): pl.pallas_call(place, out_shape=tuple((pltpu.HBM(x.shape, x.dtype) for x...  2.33 us

profile of v8, /device:TPU:1, one launch (start us, length us, event | category | flops | bytes accessed | tf_op | source)
XLA Modules:
  0.0 91.8 jit_solution(3828135217445770305)
XLA Ops:
  0.6 88.8 %migrate.1 = (bf16[32,2,4096]{2,1,0:T(2,128)(2,1)S(1)}, bf16[32,2,2,128,128]{4,3,2,1,0:T(8,128)(2,1)S(1)}, bf16[32,4096]{1,0:T(8,128)(2,1)S(1)}) custom-call(s32[32]{0:T(128)} %lens.1, s32[32]{0:T(128)} %tgts.1, s32[32]{0:T(128)} %mig.1, s32[2,32]{1,0:T(2,128)} %bitcast.1, bf16[32,2,512]{2,1,0:T(2,128)(2,1)} %qsrc.1, bf16[32,2,2,128]{3,2,1,0:T(2,128)(2,1)} %fresh.1, ...), custom_call_target="tpu_custom_call" | custom-call | tf_op jit(solution)/shard_map/migrate/pallas_call | solution.py:596
  89.4 2.3 %place.1 = (bf16[32,2,4096]{2,1,0:T(2,128)(2,1)}, bf16[32,2,2,128,128]{4,3,2,1,0:T(8,128)(2,1)}, bf16[32,4096]{1,0:T(8,128)(2,1)}) custom-call(bf16[32,2,4096]{2,1,0:T(2,128)(2,1)S(1)} %get-tuple-element.6.src_in, bf16[32,2,2,128,128]{4,3,2,1,0:T(8,128)(2,1)S(1)} %get-tuple-element.7.cache_in, bf16[32,4096]{1,0:T(8,128)(2,1)S(1)} %get-tuple-element.8.dst_in), custom_call_target="tpu_custom_call" | custom-call | tf_op jit(solution)/shard_map/place/pallas_call | solution.py:647

commit v9 on v6

--- a/solution.py
+++ b/solution.py
@@ -54,15 +54,19 @@
     tgts,
     mig,
     table,
-    qsrc,
-    fresh,
-    qdst,
-    rdst,
+    qsrc_hbm,
+    fresh_hbm,
+    qdst_hbm,
+    rdst_hbm,
     pool_hbm,
     w_hbm,
     s_full,
     cache_out,
     d_full,
+    qsrc,
+    fresh,
+    qdst,
+    rdst,
     pool,
     w,
     send,
@@ -109,7 +113,15 @@
 
     load_pool = pltpu.make_async_copy(pool_hbm, pool, load_sem.at[0])
     load_w = pltpu.make_async_copy(w_hbm, w, load_sem.at[1])
+    small = [
+        pltpu.make_async_copy(src, dst, load_sem.at[2 + i])
+        for i, (src, dst) in enumerate(
+            ((fresh_hbm, fresh), (qsrc_hbm, qsrc), (qdst_hbm, qdst), (rdst_hbm, rdst))
+        )
+    ]
     load_pool.start()
+    for copy in small:
+        copy.start()
     barrier = pltpu.get_barrier_semaphore()
 
     def greet(k, _):
@@ -180,6 +192,8 @@
             end = jnp.where(tile_row == TILE - 1.0, length if c == 0 else flag, end)
             ref[slot, 1, c, PAGE - TILE :] = end.astype(BF16)
 
+    for copy in small:
+        copy.wait()
     q_wide = qsrc[...].astype(F32)
     for g in range(GROUPS):
         lanes = slice(g * HEAD, (g + 1) * HEAD)
@@ -452,10 +466,10 @@
         flag = arr[slot, 1, 1, PAGE - TILE :].astype(F32)[TILE - 1 :]
         return length, flag == 1.0
 
-    def dst_step(b, _):
+    def attend_items(start, count):
         slots, parts0, parts1, values = [], [], [], []
-        for i in range(batch):
-            k = b * batch + i
+        for i in range(count):
+            k = start + i
 
             @pl.when(k > 0)
             def _():
@@ -465,15 +479,15 @@
             def _():
                 launch(k + ahead)
 
-        for i in range(batch):
-            k = b * batch + i
+        for i in range(count):
+            k = start + i
 
             @pl.when(k > 0)
             def _():
                 arrive(k).wait_recv()
 
-        for i in range(batch):
-            slot = partner(b * batch + i)
+        for i in range(count):
+            slot = partner(start + i)
             slots.append(slot)
             length, moved = state(slot)
             own = rdst[slot].astype(F32)
@@ -486,12 +500,19 @@
             keep1 = (lane4 + float(PAGE) < length) | (lane4 >= PAGE - 3.0)
             parts1.append(jnp.where(keep1, s1, NEG))
             values.append((arr[slot, 0, 1], value1, moved))
-        for i in range(batch):
+        for i in range(count):
             w0, w1 = soft(parts0[i], parts1[i])
             mixed = dot(w0, values[i][0]) + dot(w1, values[i][1])
             mixed = jnp.where(values[i][2], mixed, 0.0)
             for g in range(GROUPS):
                 att_d[g, pl.ds(slots[i], 1), :] = mixed[g : g + 1]
+
+    def dst_step(b, _):
+        attend_items(b * batch, batch)
+        return 0
+
+    def last_step(b, _):
+        attend_items(b * 2 * batch, 2 * batch)
         return 0
 
     def fill_step(b, _):
@@ -530,7 +551,7 @@
     lax.fori_loop(marks[2], marks[3], both, 0)
     total_up()
     lax.fori_loop(marks[3], marks[4], both, 0)
-    lax.fori_loop(marks[4], marks[6], dst_step, 0)
+    lax.fori_loop(marks[4] // 2, marks[6] // 2, last_step, 0)
 
     dst_tail = tail(1, att_d, d_half, d_half_in, d_pair, d_rs, d_rs_in, d_full)
     dst_tail[0]()
@@ -601,9 +622,13 @@
             pltpu.VMEM(cache, BF16),
             pltpu.VMEM((requests, width), BF16),
         ),
-        in_specs=[smem] * 4 + [vmem] * 4 + [hbm] * 2,
+        in_specs=[smem] * 4 + [hbm] * 6,
         out_specs=(vmem, vmem, vmem),
         scratch_shapes=[
+            pltpu.VMEM(queries_src.shape, BF16),
+            pltpu.VMEM(new_rows.shape, BF16),
+            pltpu.VMEM(queries_dst.shape, BF16),
+            pltpu.VMEM(rows_dst.shape, BF16),
             pltpu.VMEM(pool.shape, BF16),
             pltpu.VMEM(w_out.shape, BF16),
             pltpu.VMEM(cache, BF16),
@@ -616,7 +641,7 @@
         + sums(2 * requests, [(2, cols // 2)] * 2 + [(2, cols)] * 2)
         + sums(requests, [(his, cols)] * 2)
         + [
-            dma((2,)),
+            dma((6,)),
             dma((n,)),
             dma((n,)),
             dma((4,)),

time: 90 us -> 88.9 us (0.988)
  Pallas kernels: 89.3 us -> 88.2 us
    pallas_call x1, Pallas kernels: 86.9 us -> 85.8 us  [shards(): pl.pallas_call(functools.partial(kernel, n, tp_size), out_shape=(pltpu.VM...]
where the time goes in v9:
time: 88.9 us; the launch traced here: 88.8 us
  Pallas kernels  88.2 us (99%)
    pallas_call x1, Pallas kernels, shards(): pl.pallas_call(functools.partial(kernel, n, tp_size), out_shape=(pltpu.VM...  85.8 us
    pallas_call x1, Pallas kernels, shards(): pl.pallas_call(place, out_shape=tuple((pltpu.HBM(x.shape, x.dtype) for x...  2.33 us

profile of v9, /device:TPU:1, one launch (start us, length us, event | category | flops | bytes accessed | tf_op | source)
XLA Modules:
  0.0 88.8 jit_solution(7182229991662164840)
XLA Ops:
  0.6 85.8 %migrate.1 = (bf16[32,2,4096]{2,1,0:T(2,128)(2,1)S(1)}, bf16[32,2,2,128,128]{4,3,2,1,0:T(8,128)(2,1)S(1)}, bf16[32,4096]{1,0:T(8,128)(2,1)S(1)}) custom-call(s32[32]{0:T(128)} %lens.1, s32[32]{0:T(128)} %tgts.1, s32[32]{0:T(128)} %mig.1, s32[2,32]{1,0:T(2,128)} %bitcast.1, bf16[32,2,512]{2,1,0:T(2,128)(2,1)} %qsrc_hbm.1, bf16[32,2,2,128]{3,2,1,0:T(2,128)(2,1)} %fresh_hbm.1, ...), custom_call_target="tpu_custom_call" | custom-call | tf_op jit(solution)/shard_map/migrate/pallas_call | solution.py:618
  86.5 2.3 %place.1 = (bf16[32,2,4096]{2,1,0:T(2,128)(2,1)}, bf16[32,2,2,128,128]{4,3,2,1,0:T(8,128)(2,1)}, bf16[32,4096]{1,0:T(8,128)(2,1)}) custom-call(bf16[32,2,4096]{2,1,0:T(2,128)(2,1)S(1)} %get-tuple-element.6.src_in, bf16[32,2,2,128,128]{4,3,2,1,0:T(8,128)(2,1)S(1)} %get-tuple-element.7.cache_in, bf16[32,4096]{1,0:T(8,128)(2,1)S(1)} %get-tuple-element.8.dst_in), custom_call_target="tpu_custom_call" | custom-call | tf_op jit(solution)/shard_map/place/pallas_call | solution.py:673

commit v10 on v9

--- a/solution.py
+++ b/solution.py
@@ -17,6 +17,7 @@
 GROUPS = 4
 TILE = 16
 PIECES = 8
+SWAPS = ((1, 21), (2, 20), (24, 18))
 MIX = 11
 
 
@@ -27,6 +28,10 @@
         u, v = (a // weight) % 2, (b // weight) % 2
         total = total + (u + v - 2 * u * v) * weight
     return total
+
+
+def same(a, b):
+    return 1 - ((a - b) * (a - b) + 1023) // 1024
 
 
 def order(k, n):
@@ -44,7 +49,10 @@
     plane1 = 6 + 5 * turn + spot - spot // 3 - 1
     count = hop * ((1 - late) * cross0 + late * cross1)
     count = count + (1 - hop) * ((1 - late) * plane0 + late * plane1)
-    return ((count * MIX) % 16) * 2 + hop
+    peer = ((count * MIX) % 16) * 2 + hop
+    for one, other in SWAPS:
+        peer = peer + (same(peer, one) - same(peer, other)) * (other - one)
+    return peer
 
 
 def kernel(

time: 88.9 us -> 90.7 us (1.020)
  Pallas kernels: 88.2 us -> 89.9 us
    pallas_call x1, Pallas kernels: 85.8 us -> 87.6 us  [shards(): pl.pallas_call(functools.partial(kernel, n, tp_size), out_shape=(pltpu.VM...]
where the time goes in v10:
time: 90.7 us; the launch traced here: 90.6 us
  Pallas kernels  89.9 us (99%)
    pallas_call x1, Pallas kernels, shards(): pl.pallas_call(functools.partial(kernel, n, tp_size), out_shape=(pltpu.VM...  87.6 us
    pallas_call x1, Pallas kernels, shards(): pl.pallas_call(place, out_shape=tuple((pltpu.HBM(x.shape, x.dtype) for x...  2.33 us

profile of v10, /device:TPU:1, one launch (start us, length us, event | category | flops | bytes accessed | tf_op | source)
XLA Modules:
  0.0 90.6 jit_solution(1898397323882969541)
XLA Ops:
  0.6 87.6 %migrate.1 = (bf16[32,2,4096]{2,1,0:T(2,128)(2,1)S(1)}, bf16[32,2,2,128,128]{4,3,2,1,0:T(8,128)(2,1)S(1)}, bf16[32,4096]{1,0:T(8,128)(2,1)S(1)}) custom-call(s32[32]{0:T(128)} %lens.1, s32[32]{0:T(128)} %tgts.1, s32[32]{0:T(128)} %mig.1, s32[2,32]{1,0:T(2,128)} %bitcast.1, bf16[32,2,512]{2,1,0:T(2,128)(2,1)} %qsrc_hbm.1, bf16[32,2,2,128]{3,2,1,0:T(2,128)(2,1)} %fresh_hbm.1, ...), custom_call_target="tpu_custom_call" | custom-call | tf_op jit(solution)/shard_map/migrate/pallas_call | solution.py:626
  88.2 2.3 %place.1 = (bf16[32,2,4096]{2,1,0:T(2,128)(2,1)}, bf16[32,2,2,128,128]{4,3,2,1,0:T(8,128)(2,1)}, bf16[32,4096]{1,0:T(8,128)(2,1)}) custom-call(bf16[32,2,4096]{2,1,0:T(2,128)(2,1)S(1)} %get-tuple-element.6.src_in, bf16[32,2,2,128,128]{4,3,2,1,0:T(8,128)(2,1)S(1)} %get-tuple-element.7.cache_in, bf16[32,4096]{1,0:T(8,128)(2,1)S(1)} %get-tuple-element.8.dst_in), custom_call_target="tpu_custom_call" | custom-call | tf_op jit(solution)/shard_map/place/pallas_call | solution.py:681
